TPU v7x, 32 devices: a whole 2x2x4 slice. The times are simulated.
32 devices in a mesh: section: 8 (over z, x), ctx: 4 (over y, core).
Axes of the slice: x: 2, y: 2, z: 4, core: 2. Of those that a mesh axis runs over, the one named last changes fastest.
Arguments:
- queries: bfloat16 [8, 1024, 16, 128], P('section', 'ctx'), may hold values from -12 to 12
- keys: bfloat16 [8, 1024, 128], P('section', 'ctx'), may hold values from -6 to 6
- values: bfloat16 [8, 1024, 128], P('section', 'ctx'), may hold values from -6 to 6
- outputs: bfloat16 [8, 1024, 16, 128], P('section', 'ctx'), may hold values from -6 to 6, as said below
- grad_held: bfloat16 [8, 1024, 16, 128], P('section', 'ctx'), may hold values from -24 to 24
- lse: float32 [8, 16, 1024], P('section', None, 'ctx'), as said below
- span_start: int32 [8], replicated, may hold values from 0 to 896, as said below
Outputs:
- query_grad: bfloat16 [8, 1024, 16, 128], P('section', 'ctx')
- key_grad: bfloat16 [8, 1024, 128], P('section', 'ctx')
- value_grad: bfloat16 [8, 1024, 128], P('section', 'ctx')
Inputs may be any that keep to these rules, and one draw needn't show every extreme that they name: `span_start`: each multiple of 128 below 1024 appears once. Entries 2 k and 2 k + 1 are the spans held by index k of ctx; they add up to 896, the smaller first. lse[s, h, i] is the log of the sum of exp(scores[s, h, i, j]) over the j with positions[j] <= positions[i]. outputs[s, i, h] is the sum over j of probs[s, h, i, j] values[s, j], rounded once.
All inputs are finite; a program needn't handle non-finite values.
Results may differ from a plain program's by a relative error of at most 0.014.
Values may be sent and summed in bfloat16 or wider, within the bound.
No kernel may reach another device: no remote copies, remote signals or barrier semaphores. Data moves between devices by JAX's collectives and lax.ppermute only.
A program may use at most 64 MiB of HBM per device.

v0:
```python
import functools
import math

import jax
import jax.numpy as jnp
from jax import lax
from jax.experimental import pallas as pl
from jax.experimental.pallas import tpu as pltpu
from jax.sharding import PartitionSpec as P

KEY_BLOCK = 512
LANES = 128
UPPER_CHUNKS = (64, 64)
LOWER_CHUNKS = (80, 48)
VMEM_LIMIT = 40 * 1024 * 1024
SORT_FLOPS = 10**9
WIDEN_FLOPS = 4 * 10**9

WHOLE = pl.BlockSpec(memory_space=pltpu.VMEM)
SCALARS = pl.BlockSpec(memory_space=pltpu.SMEM)
ANYWHERE = pl.BlockSpec(memory_space=pl.ANY)
NT = (((1,), (1,)), ((), ()))


def from_behind(shard, axis, by):
    length = lax.axis_size(axis)
    return lax.ppermute(shard, axis, [(i, (i + by) % length) for i in range(length)])


def with_partner(shard, axis, step):
    length = lax.axis_size(axis)
    return lax.ppermute(shard, axis, [(i, i ^ step) for i in range(length)])


def params(limit=VMEM_LIMIT):
    return pltpu.CompilerParams(vmem_limit_bytes=limit)


def cut_kernel(cuts, source_ref, *refs):
    *out_refs, sems = refs
    copies = [
        pltpu.make_async_copy(source_ref.at[pl.ds(first, size)], out_ref, sems.at[i])
        for i, ((first, size), out_ref) in enumerate(zip(cuts, out_refs))
    ]
    for copy in copies:
        copy.start()
    for copy in copies:
        copy.wait()


def cut(source, cuts):
    return pl.pallas_call(
        functools.partial(cut_kernel, cuts),
        out_shape=[
            jax.ShapeDtypeStruct((size, *source.shape[1:]), source.dtype) for _, size in cuts
        ],
        in_specs=[ANYWHERE],
        out_specs=[ANYWHERE] * len(cuts),
        scratch_shapes=[pltpu.SemaphoreType.DMA((len(cuts),))],
        compiler_params=params(),
        cost_estimate=pl.CostEstimate(
            flops=0, bytes_accessed=2 * source.size * source.dtype.itemsize, transcendentals=0
        ),
    )(source)


def widen_kernel(rows, g_ref, o_ref, *refs):
    wide_ref = refs[-1]
    head_size = g_ref.shape[1]
    g = g_ref[...]
    wide_ref[:, :head_size] = g
    wide_ref[:, head_size:] = times(g, o_ref[rows, :])


def widen(grad, outputs, first, *others):
    row_count, head_size = grad.shape
    return pl.pallas_call(
        functools.partial(widen_kernel, slice(first, first + row_count)),
        out_shape=jax.ShapeDtypeStruct((row_count, 2 * head_size), grad.dtype),
        in_specs=[WHOLE] * (2 + len(others)),
        out_specs=WHOLE,
        compiler_params=params(),
        cost_estimate=pl.CostEstimate(
            flops=WIDEN_FLOPS, bytes_accessed=grad.size * 8, transcendentals=0
        ),
    )(grad, outputs, *others)


def times(g, o):
    return (g.astype(jnp.float32) * o.astype(jnp.float32)).astype(jnp.bfloat16)


def stack_kernel(*refs):
    *part_refs, out_ref = refs
    first = 0
    for part_ref in part_refs:
        out_ref[first : first + part_ref.shape[0]] = part_ref[...]
        first += part_ref.shape[0]


def stack(parts):
    shape = (sum(part.shape[0] for part in parts), *parts[0].shape[1:])
    return pl.pallas_call(
        stack_kernel,
        out_shape=jax.ShapeDtypeStruct(shape, parts[0].dtype),
        in_specs=[WHOLE] * len(parts),
        out_specs=WHOLE,
        compiler_params=params(),
        cost_estimate=pl.CostEstimate(flops=0, bytes_accessed=2**18, transcendentals=0),
    )(*parts)


def place_of(places_ref, step, half):
    lane = lax.broadcasted_iota(jnp.int32, places_ref.shape, 1)
    place = jnp.max(jnp.where(lane == 2 * step + half, places_ref[...], 0.0))
    return pl.multiple_of(place.astype(jnp.int32), LANES)


def sort_keys_kernel(codes, span_rows, head_size, starts_ref, *refs):
    held_ref, got_ref, keys_ref, values_ref, keys_t_ref, places_ref = refs
    half_count = len(codes) // 2
    blocks = [(ref, 2 * i) for ref in (held_ref, got_ref) for i in range(half_count)]
    me = lax.axis_index("ctx")
    lane = lax.broadcasted_iota(jnp.int32, places_ref.shape, 1)
    places = jnp.zeros(places_ref.shape, jnp.float32)
    values_ref[:, head_size:] = jnp.full(
        (values_ref.shape[0], values_ref.shape[1] - head_size), -1.0, values_ref.dtype
    )
    for (block, at), code in zip(blocks, codes):
        owner = lax.bitwise_xor(me, code)
        for half in range(2):
            start = pl.multiple_of(starts_ref[2 * owner + half], span_rows)
            rows = pl.ds(start, span_rows)
            part = slice(half * span_rows, (half + 1) * span_rows)
            keys = block[at, part, :]
            keys_ref[rows, :] = keys
            values_ref[rows, :head_size] = block[at + 1, part, :]
            keys_t_ref[:, rows] = keys.astype(jnp.float32).T.astype(jnp.bfloat16)
            places = jnp.where(lane == 2 * code + half, start.astype(jnp.float32), places)
    places_ref[...] = places


def sort_keys(span_start, blocks, codes, span_rows, head_size):
    total = len(codes) * 2 * span_rows
    return pl.pallas_call(
        functools.partial(sort_keys_kernel, codes, span_rows, head_size),
        out_shape=(
            jax.ShapeDtypeStruct((total, head_size), jnp.bfloat16),
            jax.ShapeDtypeStruct((total, 2 * head_size), jnp.bfloat16),
            jax.ShapeDtypeStruct((head_size, total), jnp.bfloat16),
            jax.ShapeDtypeStruct((8, LANES), jnp.float32),
        ),
        in_specs=[SCALARS] + [WHOLE] * len(blocks),
        out_specs=(WHOLE,) * 4,
        compiler_params=params(),
        cost_estimate=pl.CostEstimate(
            flops=SORT_FLOPS, bytes_accessed=8 * total * head_size, transcendentals=0
        ),
    )(span_start, *blocks)


def chunk_grads(
    chunk, heads, span_rows, places_ref, q_ref, g_ref, o_ref, lse_ref, keys_ref, values_ref,
    keys_t_ref, total_ref, dq_ref,
):
    half, first, tokens = chunk
    head_size = q_ref.shape[1]
    scale = head_size**-0.5
    to_log2 = math.log2(math.e)
    start = place_of(places_ref, 0, half)
    row_count = tokens * heads
    row_first = (half * span_rows + first) * heads
    rows = slice(row_first, row_first + row_count)
    full_blocks = start // KEY_BLOCK

    q = q_ref[rows, :]
    g = g_ref[...]
    if g.shape[1] == head_size:
        g_wide = jnp.concatenate([g, times(g, o_ref[rows, :])], axis=1)
    else:
        g, g_wide = g[:, :head_size], g
    lse2 = lse_ref[0:1, rows] * to_log2
    dq_ref[...] = jnp.zeros_like(dq_ref)

    def block(base, size, masked):
        base = pl.multiple_of(base, KEY_BLOCK)
        at = pl.ds(base, size)
        scores = lax.dot_general(keys_ref[at, :], q, NT, preferred_element_type=jnp.float32)
        probs = jnp.exp2(scores * (scale * to_log2) - lse2)
        if masked:
            query_row = lax.broadcasted_iota(jnp.int32, (1, row_count), 1)
            query_pos = start + first + query_row // heads
            key_pos = base + lax.broadcasted_iota(jnp.int32, (size, 1), 0)
            probs = jnp.where(key_pos <= query_pos, probs, 0.0)
        centred = lax.dot_general(values_ref[at, :], g_wide, NT, preferred_element_type=jnp.float32)
        grad_scores = (probs * centred).astype(jnp.bfloat16)
        probs_low = probs.astype(jnp.bfloat16)
        total_ref[at, :head_size] += jnp.dot(grad_scores, q, preferred_element_type=jnp.float32)
        total_ref[at, head_size:] += jnp.dot(probs_low, g, preferred_element_type=jnp.float32)
        dq_ref[...] += jnp.dot(keys_t_ref[:, at], grad_scores, preferred_element_type=jnp.float32)

    def dense(index, carry):
        block(index * KEY_BLOCK, KEY_BLOCK, False)
        return carry

    lax.fori_loop(0, full_blocks, dense, 0)
    last = full_blocks * KEY_BLOCK
    short = start - last < KEY_BLOCK // 2

    @pl.when(short)
    def _():
        block(last, KEY_BLOCK // 2, True)

    @pl.when(jnp.logical_not(short))
    def _():
        block(last, KEY_BLOCK, True)


def hand_out(half, count, span_rows, places_ref, total_ref, own_ref, send_refs):
    head_size = total_ref.shape[1] // 2
    scale = head_size**-0.5
    for step, target in enumerate([own_ref, *send_refs]):
        rows = pl.ds(place_of(places_ref, step, half), span_rows)
        target[:, :head_size] = (total_ref[rows, :head_size] * scale).astype(target.dtype)
        target[:, head_size:] = total_ref[rows, head_size:].astype(target.dtype)


def add_terms(term_refs):
    total = term_refs[0][...]
    for term_ref in term_refs[1:]:
        total = total + term_ref[...].astype(jnp.float32)
    return total


def chunk_kernel(
    chunk, heads, span_rows, count, is_first, is_last, hands_out, n_after, q_ref, g_ref, o_ref,
    lse_ref, keys_ref, values_ref, keys_t_ref, places_ref, *refs,
):
    refs = list(refs[n_after:])
    total_in = None if is_first else refs.pop(0)
    total_ref = refs.pop() if is_last else refs.pop(1)
    dq_ref, *handed = refs
    if is_first:
        total_ref[...] = jnp.zeros_like(total_ref)
    else:
        total_ref[...] = total_in[: total_ref.shape[0], :]
    chunk_grads(
        chunk, heads, span_rows, places_ref, q_ref, g_ref, o_ref, lse_ref, keys_ref, values_ref,
        keys_t_ref, total_ref, dq_ref,
    )
    if hands_out:
        hand_out(chunk[0], count, span_rows, places_ref, total_ref, handed[0], handed[1:])


def add_kernel(count, span_rows, head_size, *refs):
    term_refs, upper_ref, (key_ref, value_ref) = refs[:count], refs[count], refs[count + 1 :]
    lower = add_terms(term_refs).astype(jnp.bfloat16)
    for out_ref, columns in ((key_ref, slice(0, head_size)), (value_ref, slice(head_size, None))):
        out_ref[:span_rows, :] = lower[:, columns]
        out_ref[span_rows:, :] = upper_ref[:, columns]


def finish_kernel(count, places, *refs):
    term_refs, refs = refs[:count], refs[count:]
    part_refs, (upper_ref, out_ref, held, sems) = refs[: len(places)], refs[len(places) :]
    scale = out_ref.shape[1] ** -0.5
    copies = []
    for i, (first, part_ref) in enumerate(zip(places, part_refs)):
        rows = pl.ds(first, part_ref.shape[1])
        held[rows, :] = (part_ref[...] * scale).T.astype(jnp.bfloat16)
        copies.append(pltpu.make_async_copy(held.at[rows], out_ref.at[rows], sems.at[i]))
        copies[-1].start()
    upper_ref[...] = add_terms(term_refs).astype(jnp.bfloat16)
    for copy in copies:
        copy.wait()


def finish(terms, parts, places, shape):
    return pl.pallas_call(
        functools.partial(finish_kernel, len(terms), places),
        out_shape=(
            jax.ShapeDtypeStruct(terms[0].shape, jnp.bfloat16),
            jax.ShapeDtypeStruct(shape, jnp.bfloat16),
        ),
        in_specs=[WHOLE] * (len(terms) + len(parts)),
        out_specs=(WHOLE, ANYWHERE),
        scratch_shapes=[
            pltpu.VMEM(shape, jnp.bfloat16),
            pltpu.SemaphoreType.DMA((len(parts),)),
        ],
        compiler_params=params(),
    )(*terms, *parts)


def body(queries, keys, values, outputs, grad_held, lse, span_start):
    count = lax.axis_size("ctx")
    row_count, heads, head_size = queries.shape[1:]
    span_rows = row_count // 2
    total = count * row_count
    chunks = []
    for half, sizes in ((1, UPPER_CHUNKS), (0, LOWER_CHUNKS)):
        chunks += [(half, sum(sizes[:i]), size) for i, size in enumerate(sizes)]

    pieces = cut(grad_held[0], [(half * span_rows + first, size) for half, first, size in chunks])
    grads = [from_behind(pieces[0], "section", -1)]
    pair = jnp.concatenate(lax.optimization_barrier((keys, values, pieces[0]))[:2], axis=0)
    gathered, codes, step = pair, [0], count // 2
    while step:
        held, gathered = gathered, with_partner(gathered, "ctx", step)
        codes = codes + [code ^ step for code in codes]
        if step > 1:
            gathered = stack([held, gathered])
        step //= 2
    for piece, gate in zip(pieces[1:], [None] * (len(pieces) - 2) + [held]):
        if gate is not None:
            piece, _ = lax.optimization_barrier((piece, gate))
        grads.append(from_behind(piece, "section", -1))
    sorted_keys = sort_keys(span_start, [held, gathered], codes, span_rows, head_size)

    q_flat = queries.reshape(row_count * heads, head_size)
    o_flat = outputs.reshape(row_count * heads, head_size)
    lse_flat = lse[0].T.reshape(1, row_count * heads)

    span_wide = (span_rows, 2 * head_size)
    running, received, dq_parts = [], [], []
    for number, chunk in enumerate(chunks):
        half, _, tokens = chunk
        rows = tokens * heads
        is_first, is_last = number == 0, number == len(chunks) - 1
        hands_out = chunk[1] + tokens == span_rows
        after = received[:2] if is_last else []
        if is_last:
            upper_terms = received
        grad = grads[number].reshape(rows, head_size)
        if is_first:
            grad = widen(grad, o_flat, (half * span_rows + chunk[1]) * heads)
        operands = [
            q_flat, grad, o_flat, lse_flat, *sorted_keys, *after,
            *running,
        ]
        total_shape = (total if half else total // 2, 2 * head_size)
        out_shape = [jax.ShapeDtypeStruct((head_size, rows), jnp.float32)]
        if not is_last:
            out_shape.append(jax.ShapeDtypeStruct(total_shape, jnp.float32))
        if hands_out:
            out_shape.append(jax.ShapeDtypeStruct(span_wide, jnp.float32))
            out_shape += [jax.ShapeDtypeStruct(span_wide, jnp.bfloat16)] * (count - 1)
        pairs = rows * (3 * total // 4 if half == 1 else total // 4)
        dq, *handed = pl.pallas_call(
            functools.partial(
                chunk_kernel, chunk, heads, span_rows, count, is_first, is_last, hands_out,
                len(after),
            ),
            out_shape=out_shape,
            in_specs=[WHOLE] * len(operands),
            out_specs=[WHOLE] * len(out_shape),
            scratch_shapes=[pltpu.VMEM(total_shape, jnp.float32)] if is_last else [],
            compiler_params=params(),
            cost_estimate=pl.CostEstimate(
                flops=20 * pairs * head_size, bytes_accessed=2 * 2**20, transcendentals=pairs
            ),
        )(*operands)
        dq_parts.append(dq)
        running = [] if is_last else [handed.pop(0)]
        if hands_out:
            sends = list(enumerate(handed[1:], start=1))
            received = [with_partner(send, "ctx", step) for step, send in reversed(sends)]
            received = [handed[0]] + received[::-1]

    places = [(half * span_rows + first) * heads for half, first, _ in chunks]
    upper_sum, dq = finish(upper_terms, dq_parts, places, q_flat.shape)
    key_out, value_out = pl.pallas_call(
        functools.partial(add_kernel, count, span_rows, head_size),
        out_shape=(jax.ShapeDtypeStruct((row_count, head_size), jnp.bfloat16),) * 2,
        in_specs=[WHOLE] * (count + 1),
        out_specs=(WHOLE,) * 2,
        compiler_params=params(),
    )(*received, upper_sum)
    return (dq.reshape(queries.shape), key_out[None], value_out[None])


def solution(mesh):
    placed = (
        P("section", "ctx", None, None),
        P("section", "ctx", None),
        P("section", "ctx", None),
        P("section", "ctx", None, None),
        P("section", "ctx", None, None),
        P("section", None, "ctx"),
        P(),
    )
    return jax.shard_map(
        body,
        mesh=mesh,
        in_specs=placed,
        out_specs=(
            P("section", "ctx", None, None),
            P("section", "ctx", None),
            P("section", "ctx", None),
        ),
        check_vma=False,
    )
```

profile of v0, /device:TPU:0, one launch (start us, length us, event | category | flops | bytes accessed | tf_op | source)
XLA Modules:
  0.0 38.5 jit_solution(13205003578508123720)
XLA Ops:
  0.6 1.2 %copy-done.2 = bf16[1,256,16,128]{3,2,1,0:T(8,128)(2,1)S(1)} copy-done((bf16[1,256,16,128]{3,2,1,0:T(8,128)(2,1)S(1)}, bf16[1,256,16,128]{3,2,1,0:T(8,128)(2,1)}, u32[]{:S(2)}) %copy-start.2) | copy-done | bytes 1048600
  1.9 0.4 %shard_map.94 = (bf16[64,16,128]{2,1,0:T(8,128)(2,1)S(1)}, bf16[64,16,128]{2,1,0:T(8,128)(2,1)S(1)}, bf16[80,16,128]{2,1,0:T(8,128)(2,1)S(1)}, bf16[48,16,128]{2,1,0:T(8,128)(2,1)S(1)}) custom-call(bf16[256,16,128]{2,1,0:T(8,128)(2,1)S(1)} %bitcast.22), custom_call_target="tpu_custom_call" | custom-call | bytes 2097152 | tf_op jit(solution)/shard_map/pallas_call | solution.py:52
  2.3 6.0 %collective-permute-start.3 = (bf16[64,16,128]{2,1,0:T(8,128)(2,1)S(1)}, bf16[64,16,128]{2,1,0:T(8,128)(2,1)S(1)}, u32[]{:S(2)}, u32[]{:S(2)}) collective-permute-start(bf16[64,16,128]{2,1,0:T(8,128)(2,1)S(1)} %get-tuple-element.34), channel_id=1, source_target_pairs={{0,28},{4,0},{8,4},{12,8},{16,12},{20,16},{24,20},{28,24},{1,29},{... | collective-permute-start | bytes 786440 | tf_op jit(solution)/shard_map/ppermute | solution.py:27
  8.3 0.8 %constant_dynamic-update-slice_fusion.1 = bf16[2,256,128]{2,1,0:T(8,128)(2,1)S(1)} fusion(bf16[1,256,128]{2,1,0:T(8,128)(2,1)} %param.8), kind=kLoop, calls=%fused_computation.1 | loop fusion | bytes 131072
  9.2 1.6 %collective-permute-start.1 = (bf16[2,256,128]{2,1,0:T(8,128)(2,1)S(1)}, bf16[2,256,128]{2,1,0:T(8,128)(2,1)S(1)}, u32[]{:S(2)}, u32[]{:S(2)}) collective-permute-start(bf16[2,256,128]{2,1,0:T(8,128)(2,1)S(1)} %constant_dynamic-update-slice_fusion.refs_0_), channel_id=1, source_target_pairs={{0,2},{1,3},{2,0},{3,1},{4,6},{5,7},{6,4},{7,5},{8,10},{9,11},{10,... | collective-permute-start | bytes 393224 | tf_op jit(solution)/shard_map/ppermute | solution.py:32
  10.8 0.5 %collective-permute-start = (bf16[64,16,128]{2,1,0:T(8,128)(2,1)S(1)}, bf16[64,16,128]{2,1,0:T(8,128)(2,1)S(1)}, u32[]{:S(2)}, u32[]{:S(2)}) collective-permute-start(bf16[64,16,128]{2,1,0:T(8,128)(2,1)S(1)} %get-tuple-element.33), channel_id=1, source_target_pairs={{0,28},{4,0},{8,4},{12,8},{16,12},{20,16},{24,20},{28,24},{1,29},{... | collective-permute-start | bytes 786440 | tf_op jit(solution)/shard_map/ppermute | solution.py:27
  11.3 1.4 %collective-permute-start.7 = (bf16[80,16,128]{2,1,0:T(8,128)(2,1)S(1)}, bf16[80,16,128]{2,1,0:T(8,128)(2,1)S(1)}, u32[]{:S(2)}, u32[]{:S(2)}) collective-permute-start(bf16[80,16,128]{2,1,0:T(8,128)(2,1)S(1)} %get-tuple-element.48), channel_id=1, source_target_pairs={{0,28},{4,0},{8,4},{12,8},{16,12},{20,16},{24,20},{28,24},{1,29},{... | collective-permute-start | bytes 983048 | tf_op jit(solution)/shard_map/ppermute | solution.py:27
  12.7 0.1 copy.11
  12.8 0.1 reshape.33.lse_ref
  12.9 1.3 %collective-permute-done.1.refs_1_ = bf16[2,256,128]{2,1,0:T(8,128)(2,1)S(1)} collective-permute-done((bf16[2,256,128]{2,1,0:T(8,128)(2,1)S(1)}, bf16[2,256,128]{2,1,0:T(8,128)(2,1)S(1)}, u32[]{:S(2)}, u32[]{:S(2)}) %collective-permute-start.1) | collective-permute-done | bytes 131104 | tf_op jit(solution)/shard_map/ppermute | solution.py:32
  14.3 0.1 collective-permute-start.2
  14.3 0.6 %collective-permute-start.8 = (bf16[48,16,128]{2,1,0:T(8,128)(2,1)S(1)}, bf16[48,16,128]{2,1,0:T(8,128)(2,1)S(1)}, u32[]{:S(2)}, u32[]{:S(2)}) collective-permute-start(bf16[48,16,128]{2,1,0:T(8,128)(2,1)S(1)} %get-tuple-element.52), channel_id=1, source_target_pairs={{0,28},{4,0},{8,4},{12,8},{16,12},{20,16},{24,20},{28,24},{1,29},{... | collective-permute-start | bytes 589832 | tf_op jit(solution)/shard_map/ppermute | solution.py:27
  14.9 0.1 collective-permute-done.3
  15.1 0.1 shard_map.97.g_ref
  15.2 0.7 %collective-permute-done.2.refs_1_ = bf16[4,256,128]{2,1,0:T(8,128)(2,1)S(1)} collective-permute-done((bf16[4,256,128]{2,1,0:T(8,128)(2,1)S(1)}, bf16[4,256,128]{2,1,0:T(8,128)(2,1)S(1)}, u32[]{:S(2)}, u32[]{:S(2)}) %collective-permute-start.2) | collective-permute-done | bytes 262176 | tf_op jit(solution)/shard_map/ppermute | solution.py:32
  15.9 0.8 %shard_map.96 = (bf16[1024,128]{1,0:T(8,128)(2,1)S(1)}, bf16[1024,256]{1,0:T(8,128)(2,1)S(1)}, bf16[128,1024]{1,0:T(8,128)(2,1)S(1)}, f32[8,128]{1,0:T(8,128)S(1)}) custom-call(s32[8]{0:T(128)S(1)} %copy-done.3, bf16[4,256,128]{2,1,0:T(8,128)(2,1)S(1)} %shard_map.95.refs_0_, bf16[4,256,128]{2,1,0:T(8,128)(2,1)S(1)} %collective-permute-done.2.refs_1_), custom_call_target="tpu_custom_call" | custom-call | flops 1000000000 | bytes 1048576 | tf_op jit(solution)/shard_map/pallas_call | solution.py:145
  16.7 2.5 %shard_map.98 = (f32[128,1024]{1,0:T(8,128)S(1)}, f32[1024,256]{1,0:T(8,128)S(1)}) custom-call(bf16[4096,128]{1,0:T(8,128)(2,1)S(1)} %bitcast.13, bf16[1024,256]{1,0:T(8,128)(2,1)S(1)} %shard_map.97.g_ref, bf16[4096,128]{1,0:T(8,128)(2,1)S(1)} %bitcast.18, f32[1,4096]{1,0:T(1,128)S(1)} %reshape.33.lse_ref, bf16[1024,128]{1,0:T(8,128)(2,1)S(1)} %get-tuple-element.37.keys_ref, ...), custom_call_target="tpu_custom_call" | custom-call | flops 2013265920 | bytes 2097152 | tf_op jit(solution)/shard_map/pallas_call | solution.py:349
  19.2 1.5 %collective-permute-done = bf16[64,16,128]{2,1,0:T(8,128)(2,1)S(1)} collective-permute-done((bf16[64,16,128]{2,1,0:T(8,128)(2,1)S(1)}, bf16[64,16,128]{2,1,0:T(8,128)(2,1)S(1)}, u32[]{:S(2)}, u32[]{:S(2)}) %collective-permute-start) | collective-permute-done | bytes 262176 | tf_op jit(solution)/shard_map/ppermute | solution.py:27
  20.7 2.7 %shard_map.99 = (f32[128,1024]{1,0:T(8,128)S(1)}, f32[1024,256]{1,0:T(8,128)S(1)}, f32[128,256]{1,0:T(8,128)S(1)}, bf16[128,256]{1,0:T(8,128)(2,1)S(1)}, bf16[12...) custom-call(bf16[4096,128]{1,0:T(8,128)(2,1)S(1)} %bitcast.14, bf16[1024,128]{1,0:T(8,128)(2,1)S(1)} %bitcast.25, ...), custom_call_target="tpu_custom_call" | custom-call | flops 2013265920 | bytes 2097152 | tf_op jit(solution)/shard_map/pallas_call | solution.py:349
  23.4 0.1 collective-permute-start.4
  23.5 2.2 %collective-permute-start.5 = (bf16[128,256]{1,0:T(8,128)(2,1)S(1)}, bf16[128,256]{1,0:T(8,128)(2,1)S(1)}, u32[]{:S(2)}, u32[]{:S(2)}) collective-permute-start(bf16[128,256]{1,0:T(8,128)(2,1)S(1)} %get-tuple-element.44), channel_id=1, source_target_pairs={{0,2},{1,3},{2,0},{3,1},{4,6},{5,7},{6,4},{7,5},{8,10},{9,11},{10,... | collective-permute-start | bytes 196616 | tf_op jit(solution)/shard_map/ppermute | solution.py:32
  25.8 1.9 %collective-permute-done.7 = bf16[80,16,128]{2,1,0:T(8,128)(2,1)S(1)} collective-permute-done((bf16[80,16,128]{2,1,0:T(8,128)(2,1)S(1)}, bf16[80,16,128]{2,1,0:T(8,128)(2,1)S(1)}, u32[]{:S(2)}, u32[]{:S(2)}) %collective-permute-start.7) | collective-permute-done | bytes 327712 | tf_op jit(solution)/shard_map/ppermute | solution.py:27
  27.7 2.4 %shard_map.100 = (f32[128,1280]{1,0:T(8,128)S(1)}, f32[512,256]{1,0:T(8,128)S(1)}) custom-call(bf16[4096,128]{1,0:T(8,128)(2,1)S(1)} %bitcast.15, bf16[1280,128]{1,0:T(8,128)(2,1)S(1)} %bitcast.23, bf16[4096,128]{1,0:T(8,128)(2,1)S(1)} %bitcast.20, f32[1,4096]{1,0:T(1,128)S(1)} %reshape.33.lse_ref, bf16[1024,128]{1,0:T(8,128)(2,1)S(1)} %get-tuple-element.37.keys_ref, ...), custom_call_target="tpu_custom_call" | custom-call | flops 838860800 | bytes 2097152 | tf_op jit(solution)/shard_map/pallas_call | solution.py:349
  30.1 0.7 %collective-permute-done.8 = bf16[48,16,128]{2,1,0:T(8,128)(2,1)S(1)} collective-permute-done((bf16[48,16,128]{2,1,0:T(8,128)(2,1)S(1)}, bf16[48,16,128]{2,1,0:T(8,128)(2,1)S(1)}, u32[]{:S(2)}, u32[]{:S(2)}) %collective-permute-start.8) | collective-permute-done | bytes 196640 | tf_op jit(solution)/shard_map/ppermute | solution.py:27
  30.8 1.5 %shard_map.101 = (f32[128,768]{1,0:T(8,128)S(1)}, f32[128,256]{1,0:T(8,128)S(1)}, bf16[128,256]{1,0:T(8,128)(2,1)S(1)}, bf16[128,256]{1,0:T(8,128)(2,1)S(1)}, bf16[128,256]{1,0:T(8,128)(2,1)S(1)}) custom-call(bf16[4096,128]{1,0:T(8,128)(2,1)S(1)} %bitcast.16, bf16[768,128]{1,0:T(8,128)(2,1)S(1)} %bitcast.24, bf16[4096,128]{1,0:T(8,128)(2,1)S(1)} %bitcast.21, ...), custom_call_target="tpu_custom_call" | custom-call | flops 503316480 | bytes 2097152 | tf_op jit(solution)/shard_map/pallas_call | solution.py:349
  32.3 0.1 collective-permute-start.9
  32.4 1.1 %collective-permute-start.10 = (bf16[128,256]{1,0:T(8,128)(2,1)S(1)}, bf16[128,256]{1,0:T(8,128)(2,1)S(1)}, u32[]{:S(2)}, u32[]{:S(2)}) collective-permute-start(bf16[128,256]{1,0:T(8,128)(2,1)S(1)} %get-tuple-element.58), channel_id=1, source_target_pairs={{0,2},{1,3},{2,0},{3,1},{4,6},{5,7},{6,4},{7,5},{8,10},{9,11},{10,... | collective-permute-start | bytes 196616 | tf_op jit(solution)/shard_map/ppermute | solution.py:32
  33.5 0.8 %collective-permute-start.11 = (bf16[128,256]{1,0:T(8,128)(2,1)S(1)}, bf16[128,256]{1,0:T(8,128)(2,1)S(1)}, u32[]{:S(2)}, u32[]{:S(2)}) collective-permute-start(bf16[128,256]{1,0:T(8,128)(2,1)S(1)} %get-tuple-element.59), channel_id=1, source_target_pairs={{0,3},{1,2},{2,1},{3,0},{4,7},{5,6},{6,5},{7,4},{8,11},{9,10},{10,... | collective-permute-start | bytes 196616 | tf_op jit(solution)/shard_map/ppermute | solution.py:32
  34.3 1.1 %shard_map.102 = (bf16[128,256]{1,0:T(8,128)(2,1)S(1)}, bf16[4096,128]{1,0:T(8,128)(2,1)}) custom-call(f32[128,256]{1,0:T(8,128)S(1)} %get-tuple-element.42.refs_0_, bf16[128,256]{1,0:T(8,128)(2,1)S(1)} %collective-permute-done.4.refs_1_, bf16[128,256]{1,0:T(8,128)(2,1)S(1)} %collective-permute-done.5.refs_2_, ...), custom_call_target="tpu_custom_call" | custom-call | tf_op jit(solution)/shard_map/pallas_call | solution.py:279
  35.4 1.9 %collective-permute-done.10.refs_2_ = bf16[128,256]{1,0:T(8,128)(2,1)S(1)} collective-permute-done((bf16[128,256]{1,0:T(8,128)(2,1)S(1)}, bf16[128,256]{1,0:T(8,128)(2,1)S(1)}, u32[]{:S(2)}, u32[]{:S(2)}) %collective-permute-start.10) | collective-permute-done | bytes 65568 | tf_op jit(solution)/shard_map/ppermute | solution.py:32
  37.3 0.5 %collective-permute-done.11.refs_3_ = bf16[128,256]{1,0:T(8,128)(2,1)S(1)} collective-permute-done((bf16[128,256]{1,0:T(8,128)(2,1)S(1)}, bf16[128,256]{1,0:T(8,128)(2,1)S(1)}, u32[]{:S(2)}, u32[]{:S(2)}) %collective-permute-start.11) | collective-permute-done | bytes 65568 | tf_op jit(solution)/shard_map/ppermute | solution.py:32
  37.9 0.7 %shard_map.103 = (bf16[256,128]{1,0:T(8,128)(2,1)}, bf16[256,128]{1,0:T(8,128)(2,1)}) custom-call(f32[128,256]{1,0:T(8,128)S(1)} %get-tuple-element.56.refs_0_, bf16[128,256]{1,0:T(8,128)(2,1)S(1)} %collective-permute-done.9.refs_1_, bf16[128,256]{1,0:T(8,128)(2,1)S(1)} %collective-permute-done.10.refs_2_, ...), custom_call_target="tpu_custom_call" | custom-call | tf_op jit(solution)/shard_map/pallas_call | solution.py:372
  (18 shorter events, 0.1 us)
Async XLA Ops:
  0.6 1.2 %copy-start.2 = (bf16[1,256,16,128]{3,2,1,0:T(8,128)(2,1)S(1)}, bf16[1,256,16,128]{3,2,1,0:T(8,128)(2,1)}, u32[]{:S(2)}) copy-start(bf16[1,256,16,128]{3,2,1,0:T(8,128)(2,1)} %param.11) | copy-start | bytes 3145732
  1.9 13.2 %copy-start.1 = (bf16[1,256,16,128]{3,2,1,0:T(8,128)(2,1)S(1)}, bf16[1,256,16,128]{3,2,1,0:T(8,128)(2,1)}, u32[]{:S(2)}) copy-start(bf16[1,256,16,128]{3,2,1,0:T(8,128)(2,1)} %param.10) | copy-start | bytes 3145732
  2.3 6.9 %copy-start.4 = (bf16[1,256,128]{2,1,0:T(8,128)(2,1)S(1)}, bf16[1,256,128]{2,1,0:T(8,128)(2,1)}, u32[]{:S(2)}) copy-start(bf16[1,256,128]{2,1,0:T(8,128)(2,1)} %param.9) | copy-start | bytes 196612
  2.3 12.7 %collective-permute-start.3 = (bf16[64,16,128]{2,1,0:T(8,128)(2,1)S(1)}, bf16[64,16,128]{2,1,0:T(8,128)(2,1)S(1)}, u32[]{:S(2)}, u32[]{:S(2)}) collective-permute-start(bf16[64,16,128]{2,1,0:T(8,128)(2,1)S(1)} %get-tuple-element.34), channel_id=1, source_target_pairs={{0,28},{4,0},{8,4},{12,8},{16,12},{20,16},{24,20},{28,24},{1,29},{... | collective-permute-start | bytes 786440 | tf_op jit(solution)/shard_map/ppermute | solution.py:27
  9.2 3.5 %copy-start.5 = (f32[1,16,256]{2,1,0:T(8,128)S(1)}, f32[1,16,256]{2,1,0:T(8,128)}, u32[]{:S(2)}) copy-start(f32[1,16,256]{2,1,0:T(8,128)} %param.12) | copy-start | bytes 49156
  9.2 5.0 %collective-permute-start.1 = (bf16[2,256,128]{2,1,0:T(8,128)(2,1)S(1)}, bf16[2,256,128]{2,1,0:T(8,128)(2,1)S(1)}, u32[]{:S(2)}, u32[]{:S(2)}) collective-permute-start(bf16[2,256,128]{2,1,0:T(8,128)(2,1)S(1)} %constant_dynamic-update-slice_fusion.refs_0_), channel_id=1, source_target_pairs={{0,2},{1,3},{2,0},{3,1},{4,6},{5,7},{6,4},{7,5},{8,10},{9,11},{10,... | collective-permute-start | bytes 393224 | tf_op jit(solution)/shard_map/ppermute | solution.py:32
  10.8 9.9 %collective-permute-start = (bf16[64,16,128]{2,1,0:T(8,128)(2,1)S(1)}, bf16[64,16,128]{2,1,0:T(8,128)(2,1)S(1)}, u32[]{:S(2)}, u32[]{:S(2)}) collective-permute-start(bf16[64,16,128]{2,1,0:T(8,128)(2,1)S(1)} %get-tuple-element.33), channel_id=1, source_target_pairs={{0,28},{4,0},{8,4},{12,8},{16,12},{20,16},{24,20},{28,24},{1,29},{... | collective-permute-start | bytes 786440 | tf_op jit(solution)/shard_map/ppermute | solution.py:27
  11.3 16.3 %collective-permute-start.7 = (bf16[80,16,128]{2,1,0:T(8,128)(2,1)S(1)}, bf16[80,16,128]{2,1,0:T(8,128)(2,1)S(1)}, u32[]{:S(2)}, u32[]{:S(2)}) collective-permute-start(bf16[80,16,128]{2,1,0:T(8,128)(2,1)S(1)} %get-tuple-element.48), channel_id=1, source_target_pairs={{0,28},{4,0},{8,4},{12,8},{16,12},{20,16},{24,20},{28,24},{1,29},{... | collective-permute-start | bytes 983048 | tf_op jit(solution)/shard_map/ppermute | solution.py:27
  14.3 1.6 %collective-permute-start.2 = (bf16[4,256,128]{2,1,0:T(8,128)(2,1)S(1)}, bf16[4,256,128]{2,1,0:T(8,128)(2,1)S(1)}, u32[]{:S(2)}, u32[]{:S(2)}) collective-permute-start(bf16[4,256,128]{2,1,0:T(8,128)(2,1)S(1)} %shard_map.95.refs_0_), channel_id=1, source_target_pairs={{0,1},{1,0},{2,3},{3,2},{4,5},{5,4},{6,7},{7,6},{8,9},{9,8},{10,11... | collective-permute-start | bytes 786440 | tf_op jit(solution)/shard_map/ppermute | solution.py:32
  14.3 16.4 %collective-permute-start.8 = (bf16[48,16,128]{2,1,0:T(8,128)(2,1)S(1)}, bf16[48,16,128]{2,1,0:T(8,128)(2,1)S(1)}, u32[]{:S(2)}, u32[]{:S(2)}) collective-permute-start(bf16[48,16,128]{2,1,0:T(8,128)(2,1)S(1)} %get-tuple-element.52), channel_id=1, source_target_pairs={{0,28},{4,0},{8,4},{12,8},{16,12},{20,16},{24,20},{28,24},{1,29},{... | collective-permute-start | bytes 589832 | tf_op jit(solution)/shard_map/ppermute | solution.py:27
  15.1 0.8 %copy-start.3 = (s32[8]{0:T(128)S(1)}, s32[8]{0:T(128)}, u32[]{:S(2)}) copy-start(s32[8]{0:T(128)} %starts_ref.1) | copy-start | bytes 100
  15.2 1.5 %copy-start = (bf16[1,256,16,128]{3,2,1,0:T(8,128)(2,1)S(1)}, bf16[1,256,16,128]{3,2,1,0:T(8,128)(2,1)}, u32[]{:S(2)}) copy-start(bf16[1,256,16,128]{3,2,1,0:T(8,128)(2,1)} %param.7) | copy-start | bytes 3145732
  23.4 7.4 %collective-permute-start.4 = (bf16[128,256]{1,0:T(8,128)(2,1)S(1)}, bf16[128,256]{1,0:T(8,128)(2,1)S(1)}, u32[]{:S(2)}, u32[]{:S(2)}) collective-permute-start(bf16[128,256]{1,0:T(8,128)(2,1)S(1)} %get-tuple-element.43), channel_id=1, source_target_pairs={{0,1},{1,0},{2,3},{3,2},{4,5},{5,4},{6,7},{7,6},{8,9},{9,8},{10,11... | collective-permute-start | bytes 196616 | tf_op jit(solution)/shard_map/ppermute | solution.py:32
  23.5 10.8 %collective-permute-start.5 = (bf16[128,256]{1,0:T(8,128)(2,1)S(1)}, bf16[128,256]{1,0:T(8,128)(2,1)S(1)}, u32[]{:S(2)}, u32[]{:S(2)}) collective-permute-start(bf16[128,256]{1,0:T(8,128)(2,1)S(1)} %get-tuple-element.44), channel_id=1, source_target_pairs={{0,2},{1,3},{2,0},{3,1},{4,6},{5,7},{6,4},{7,5},{8,10},{9,11},{10,... | collective-permute-start | bytes 196616 | tf_op jit(solution)/shard_map/ppermute | solution.py:32
  25.7 8.6 %collective-permute-start.6 = (bf16[128,256]{1,0:T(8,128)(2,1)S(1)}, bf16[128,256]{1,0:T(8,128)(2,1)S(1)}, u32[]{:S(2)}, u32[]{:S(2)}) collective-permute-start(bf16[128,256]{1,0:T(8,128)(2,1)S(1)} %get-tuple-element.45), channel_id=1, source_target_pairs={{0,3},{1,2},{2,1},{3,0},{4,7},{5,6},{6,5},{7,4},{8,11},{9,10},{10,... | collective-permute-start | bytes 196616 | tf_op jit(solution)/shard_map/ppermute | solution.py:32
  32.3 3.1 %collective-permute-start.9 = (bf16[128,256]{1,0:T(8,128)(2,1)S(1)}, bf16[128,256]{1,0:T(8,128)(2,1)S(1)}, u32[]{:S(2)}, u32[]{:S(2)}) collective-permute-start(bf16[128,256]{1,0:T(8,128)(2,1)S(1)} %get-tuple-element.57), channel_id=1, source_target_pairs={{0,1},{1,0},{2,3},{3,2},{4,5},{5,4},{6,7},{7,6},{8,9},{9,8},{10,11... | collective-permute-start | bytes 196616 | tf_op jit(solution)/shard_map/ppermute | solution.py:32
  32.4 4.9 %collective-permute-start.10 = (bf16[128,256]{1,0:T(8,128)(2,1)S(1)}, bf16[128,256]{1,0:T(8,128)(2,1)S(1)}, u32[]{:S(2)}, u32[]{:S(2)}) collective-permute-start(bf16[128,256]{1,0:T(8,128)(2,1)S(1)} %get-tuple-element.58), channel_id=1, source_target_pairs={{0,2},{1,3},{2,0},{3,1},{4,6},{5,7},{6,4},{7,5},{8,10},{9,11},{10,... | collective-permute-start | bytes 196616 | tf_op jit(solution)/shard_map/ppermute | solution.py:32
  33.5 4.4 %collective-permute-start.11 = (bf16[128,256]{1,0:T(8,128)(2,1)S(1)}, bf16[128,256]{1,0:T(8,128)(2,1)S(1)}, u32[]{:S(2)}, u32[]{:S(2)}) collective-permute-start(bf16[128,256]{1,0:T(8,128)(2,1)S(1)} %get-tuple-element.59), channel_id=1, source_target_pairs={{0,3},{1,2},{2,1},{3,0},{4,7},{5,6},{6,5},{7,4},{8,11},{9,10},{10,... | collective-permute-start | bytes 196616 | tf_op jit(solution)/shard_map/ppermute | solution.py:32
where the time goes:
time: 38.8 us; the launch traced here: 38.5 us
  starting transfers between devices  14.5 us (37%)
  Pallas kernels  12.3 us (32%)
  waiting for transfers between devices  8.65 us (22%)
  local copies, waits for them, and re-layouts  2.31 us (6%)
  between operations  0.79 us (2%)
    pallas_call x4, Pallas kernels, body(): pl.pallas_call(functools.partial(chunk_kernel, chunk, heads, span_rows, c...  9.12 us
    ppermute x4, starting transfers between devices, from_behind(): lax.ppermute(shard, axis, [(i, (i + by) % length) for i in range(length)])  8.53 us
    ppermute x8, starting transfers between devices, with_partner(): return lax.ppermute(shard, axis, [(i, i ^ step) for i in range(length)])  5.97 us
    ppermute x8, waiting for transfers between devices, with_partner(): return lax.ppermute(shard, axis, [(i, i ^ step) for i in range(length)])  4.44 us
    ppermute x4, waiting for transfers between devices, from_behind(): lax.ppermute(shard, axis, [(i, (i + by) % length) for i in range(length)])  4.21 us
    unnamed x13, local copies, waits for them, and re-layouts  2.09 us
    pallas_call x1, Pallas kernels, finish(): pl.pallas_call(functools.partial(finish_kernel, len(terms), places), out_...  1.13 us
    pallas_call x1, Pallas kernels, sort_keys(): pl.pallas_call(functools.partial(sort_keys_kernel, codes, span_rows, head...  0.79 us
  transfers between devices with their start and end apart: 12, of which 8 were waited for; matrix products, arithmetic and copies ran while one was open for 3% of the time, Pallas kernels for 29%

commit v1 on v0

--- a/solution.py
+++ b/solution.py
@@ -10,7 +10,8 @@
 
 KEY_BLOCK = 512
 LANES = 128
-UPPER_CHUNKS = (64, 64)
+TILE_TOKENS = 64
+UPPER_CHUNKS = (128,)
 LOWER_CHUNKS = (80, 48)
 VMEM_LIMIT = 40 * 1024 * 1024
 SORT_FLOPS = 10**9
@@ -117,7 +118,7 @@
 
 
 def sort_keys_kernel(codes, span_rows, head_size, starts_ref, *refs):
-    held_ref, got_ref, keys_ref, values_ref, keys_t_ref, places_ref = refs
+    held_ref, got_ref, _, keys_ref, values_ref, keys_t_ref, places_ref = refs
     half_count = len(codes) // 2
     blocks = [(ref, 2 * i) for ref in (held_ref, got_ref) for i in range(half_count)]
     me = lax.axis_index("ctx")
@@ -140,7 +141,7 @@
     places_ref[...] = places
 
 
-def sort_keys(span_start, blocks, codes, span_rows, head_size):
+def sort_keys(span_start, blocks, fetched, codes, span_rows, head_size):
     total = len(codes) * 2 * span_rows
     return pl.pallas_call(
         functools.partial(sort_keys_kernel, codes, span_rows, head_size),
@@ -150,20 +151,20 @@
             jax.ShapeDtypeStruct((head_size, total), jnp.bfloat16),
             jax.ShapeDtypeStruct((8, LANES), jnp.float32),
         ),
-        in_specs=[SCALARS] + [WHOLE] * len(blocks),
+        in_specs=[SCALARS] + [WHOLE] * (len(blocks) + 1),
         out_specs=(WHOLE,) * 4,
         compiler_params=params(),
         cost_estimate=pl.CostEstimate(
             flops=SORT_FLOPS, bytes_accessed=8 * total * head_size, transcendentals=0
         ),
-    )(span_start, *blocks)
-
-
-def chunk_grads(
-    chunk, heads, span_rows, places_ref, q_ref, g_ref, o_ref, lse_ref, keys_ref, values_ref,
+    )(span_start, *blocks, fetched)
+
+
+def tile_grads(
+    part, heads, span_rows, places_ref, q_ref, g_ref, o_ref, lse_ref, keys_ref, values_ref,
     keys_t_ref, total_ref, dq_ref,
 ):
-    half, first, tokens = chunk
+    half, first, tokens = part
     head_size = q_ref.shape[1]
     scale = head_size**-0.5
     to_log2 = math.log2(math.e)
@@ -244,10 +245,14 @@
         total_ref[...] = jnp.zeros_like(total_ref)
     else:
         total_ref[...] = total_in[: total_ref.shape[0], :]
-    chunk_grads(
-        chunk, heads, span_rows, places_ref, q_ref, g_ref, o_ref, lse_ref, keys_ref, values_ref,
-        keys_t_ref, total_ref, dq_ref,
-    )
+    half, first, tokens = chunk
+    tile = TILE_TOKENS if tokens % TILE_TOKENS == 0 else tokens
+    for at in range(0, tokens, tile):
+        rows = pl.ds(at * heads, tile * heads)
+        tile_grads(
+            (half, first + at, tile), heads, span_rows, places_ref, q_ref, g_ref.at[rows], o_ref,
+            lse_ref, keys_ref, values_ref, keys_t_ref, total_ref, dq_ref.at[:, rows],
+        )
     if hands_out:
         hand_out(chunk[0], count, span_rows, places_ref, total_ref, handed[0], handed[1:])
 
@@ -315,9 +320,9 @@
         if gate is not None:
             piece, _ = lax.optimization_barrier((piece, gate))
         grads.append(from_behind(piece, "section", -1))
-    sorted_keys = sort_keys(span_start, [held, gathered], codes, span_rows, head_size)
-
     q_flat = queries.reshape(row_count * heads, head_size)
+    sorted_keys = sort_keys(span_start, [held, gathered], q_flat, codes, span_rows, head_size)
+
     o_flat = outputs.reshape(row_count * heads, head_size)
     lse_flat = lse[0].T.reshape(1, row_count * heads)
 

time: 38.8 us -> 40.5 us (1.044)
  local copies, waits for them, and re-layouts: 2.31 us -> 3.87 us
    ppermute x4 -> x3, waiting for transfers between devices: 4.21 us -> 1.7 us  [from_behind(): lax.ppermute(shard, axis, [(i, (i + by) % length) for i in range(length)])]
    ppermute x8, waiting for transfers between devices: 4.44 us -> 6.61 us  [with_partner(): return lax.ppermute(shard, axis, [(i, i ^ step) for i in range(length)])]
    ppermute x8, starting transfers between devices: 5.97 us -> 6.89 us  [with_partner(): return lax.ppermute(shard, axis, [(i, i ^ step) for i in range(length)])]
    reshape x1, local copies, waits for them, and re-layouts: 0.11 us -> 1.01 us  [body(): lse_flat = lse[0].T.reshape(1, row_count * heads)]
    transpose x1, local copies, waits for them, and re-layouts: 0.1 us -> 0.75 us  [body(): lse_flat = lse[0].T.reshape(1, row_count * heads)]
    ppermute x4 -> x3, starting transfers between devices: 8.53 us -> 8.05 us  [from_behind(): lax.ppermute(shard, axis, [(i, (i + by) % length) for i in range(length)])]
    pallas_call x4 -> x3, Pallas kernels: 9.12 us -> 9 us  [body(): pl.pallas_call(functools.partial(chunk_kernel, chunk, heads, span_rows, c...]
  transfers between devices with their start and end apart: 12 -> 11, of which waited for: 8 -> 4; matrix products, arithmetic and copies ran while one was open for 3% -> 7% of each run, Pallas kernels for 29% -> 28%
where the time goes in v1:
time: 40.5 us; the launch traced here: 40.3 us
  starting transfers between devices  14.9 us (37%)
  Pallas kernels  12.4 us (31%)
  waiting for transfers between devices  8.3 us (20%)
  local copies, waits for them, and re-layouts  3.87 us (10%)
  between operations  0.8 us (2%)
    pallas_call x3, Pallas kernels, body(): pl.pallas_call(functools.partial(chunk_kernel, chunk, heads, span_rows, c...  9 us
    ppermute x3, starting transfers between devices, from_behind(): lax.ppermute(shard, axis, [(i, (i + by) % length) for i in range(length)])  8.05 us
    ppermute x8, starting transfers between devices, with_partner(): return lax.ppermute(shard, axis, [(i, i ^ step) for i in range(length)])  6.89 us
    ppermute x8, waiting for transfers between devices, with_partner(): return lax.ppermute(shard, axis, [(i, i ^ step) for i in range(length)])  6.61 us
    unnamed x13, local copies, waits for them, and re-layouts  2.09 us
    ppermute x3, waiting for transfers between devices, from_behind(): lax.ppermute(shard, axis, [(i, (i + by) % length) for i in range(length)])  1.7 us
    pallas_call x1, Pallas kernels, finish(): pl.pallas_call(functools.partial(finish_kernel, len(terms), places), out_...  1.19 us
    reshape x1, local copies, waits for them, and re-layouts, body(): lse_flat = lse[0].T.reshape(1, row_count * heads)  1.01 us
  transfers between devices with their start and end apart: 11, of which 4 were waited for; matrix products, arithmetic and copies ran while one was open for 7% of the time, Pallas kernels for 28%

profile of v1, /device:TPU:0, one launch (start us, length us, event | category | flops | bytes accessed | tf_op | source)
XLA Modules:
  0.0 40.3 jit_solution(4253369414426773311)
XLA Ops:
  0.6 1.2 %copy-done.2 = bf16[1,256,16,128]{3,2,1,0:T(8,128)(2,1)S(1)} copy-done((bf16[1,256,16,128]{3,2,1,0:T(8,128)(2,1)S(1)}, bf16[1,256,16,128]{3,2,1,0:T(8,128)(2,1)}, u32[]{:S(2)}) %copy-start.2) | copy-done | bytes 1048600
  1.9 0.4 %shard_map.94 = (bf16[128,16,128]{2,1,0:T(8,128)(2,1)S(1)}, bf16[80,16,128]{2,1,0:T(8,128)(2,1)S(1)}, bf16[48,16,128]{2,1,0:T(8,128)(2,1)S(1)}) custom-call(bf16[256,16,128]{2,1,0:T(8,128)(2,1)S(1)} %bitcast.20), custom_call_target="tpu_custom_call" | custom-call | bytes 2097152 | tf_op jit(solution)/shard_map/pallas_call | solution.py:53
  2.3 0.0 copy-start.4
  2.3 6.0 %collective-permute-start = (bf16[128,16,128]{2,1,0:T(8,128)(2,1)S(1)}, bf16[128,16,128]{2,1,0:T(8,128)(2,1)S(1)}, u32[]{:S(2)}, u32[]{:S(2)}) collective-permute-start(bf16[128,16,128]{2,1,0:T(8,128)(2,1)S(1)} %get-tuple-element.30), channel_id=1, source_target_pairs={{0,28},{4,0},{8,4},{12,8},{16,12},{20,16},{24,20},{28,24},{1,29},{... | collective-permute-start | bytes 1572872 | tf_op jit(solution)/shard_map/ppermute | solution.py:28
  8.3 0.8 %constant_dynamic-update-slice_fusion.1 = bf16[2,256,128]{2,1,0:T(8,128)(2,1)S(1)} fusion(bf16[1,256,128]{2,1,0:T(8,128)(2,1)} %param.8), kind=kLoop, calls=%fused_computation.1 | loop fusion | bytes 131072
  9.2 0.0 copy-start.5
  9.2 1.6 %collective-permute-start.1 = (bf16[2,256,128]{2,1,0:T(8,128)(2,1)S(1)}, bf16[2,256,128]{2,1,0:T(8,128)(2,1)S(1)}, u32[]{:S(2)}, u32[]{:S(2)}) collective-permute-start(bf16[2,256,128]{2,1,0:T(8,128)(2,1)S(1)} %constant_dynamic-update-slice_fusion.refs_0_), channel_id=1, source_target_pairs={{0,2},{1,3},{2,0},{3,1},{4,6},{5,7},{6,4},{7,5},{8,10},{9,11},{10,... | collective-permute-start | bytes 393224 | tf_op jit(solution)/shard_map/ppermute | solution.py:33
  10.8 3.4 %collective-permute-done.1.refs_1_ = bf16[2,256,128]{2,1,0:T(8,128)(2,1)S(1)} collective-permute-done((bf16[2,256,128]{2,1,0:T(8,128)(2,1)S(1)}, bf16[2,256,128]{2,1,0:T(8,128)(2,1)S(1)}, u32[]{:S(2)}, u32[]{:S(2)}) %collective-permute-start.1) | collective-permute-done | bytes 131104 | tf_op jit(solution)/shard_map/ppermute | solution.py:33
  14.3 0.1 collective-permute-start.2
  14.3 0.6 %collective-permute-start.6 = (bf16[80,16,128]{2,1,0:T(8,128)(2,1)S(1)}, bf16[80,16,128]{2,1,0:T(8,128)(2,1)S(1)}, u32[]{:S(2)}, u32[]{:S(2)}) collective-permute-start(bf16[80,16,128]{2,1,0:T(8,128)(2,1)S(1)} %get-tuple-element.42), channel_id=1, source_target_pairs={{0,28},{4,0},{8,4},{12,8},{16,12},{20,16},{24,20},{28,24},{1,29},{... | collective-permute-start | bytes 983048 | tf_op jit(solution)/shard_map/ppermute | solution.py:28
  14.9 0.8 %copy.11 = f32[256,16]{1,0:T(8,128)} copy(f32[256,16]{0,1:T(8,128)S(1)} %bitcast.24) | data formatting | bytes 32768 | tf_op jit(solution)/shard_map/transpose | solution.py:327
  15.7 1.0 %reshape.30.lse_ref = f32[1,4096]{1,0:T(1,128)S(1)} reshape(f32[256,16]{1,0:T(8,128)} %copy.11) | data formatting | bytes 32768 | tf_op jit(solution)/shard_map/reshape | solution.py:327
  16.7 0.0 copy-start.3
  16.7 1.4 %collective-permute-start.7 = (bf16[48,16,128]{2,1,0:T(8,128)(2,1)S(1)}, bf16[48,16,128]{2,1,0:T(8,128)(2,1)S(1)}, u32[]{:S(2)}, u32[]{:S(2)}) collective-permute-start(bf16[48,16,128]{2,1,0:T(8,128)(2,1)S(1)} %get-tuple-element.46), channel_id=1, source_target_pairs={{0,28},{4,0},{8,4},{12,8},{16,12},{20,16},{24,20},{28,24},{1,29},{... | collective-permute-start | bytes 589832 | tf_op jit(solution)/shard_map/ppermute | solution.py:28
  18.1 0.0 collective-permute-done.2.refs_1_
  18.1 0.0 copy-start.1
  18.2 0.8 %shard_map.97 = (bf16[1024,128]{1,0:T(8,128)(2,1)S(1)}, bf16[1024,256]{1,0:T(8,128)(2,1)S(1)}, bf16[128,1024]{1,0:T(8,128)(2,1)S(1)}, f32[8,128]{1,0:T(8,128)S(1)}) custom-call(s32[8]{0:T(128)S(1)} %copy-done.3, bf16[4,256,128]{2,1,0:T(8,128)(2,1)S(1)} %shard_map.96.refs_0_, bf16[4,256,128]{2,1,0:T(8,128)(2,1)S(1)} %collective-permute-done.2.refs_1_, ...), custom_call_target="tpu_custom_call" | custom-call | flops 1000000000 | bytes 1048576 | tf_op jit(solution)/shard_map/pallas_call | solution.py:146
  19.0 1.7 %collective-permute-done = bf16[128,16,128]{2,1,0:T(8,128)(2,1)S(1)} collective-permute-done((bf16[128,16,128]{2,1,0:T(8,128)(2,1)S(1)}, bf16[128,16,128]{2,1,0:T(8,128)(2,1)S(1)}, u32[]{:S(2)}, u32[]{:S(2)}) %collective-permute-start) | collective-permute-done | bytes 524320 | tf_op jit(solution)/shard_map/ppermute | solution.py:28
  20.7 0.3 shard_map.95.g_ref
  20.9 5.1 %shard_map.98 = (f32[128,2048]{1,0:T(8,128)S(1)}, f32[1024,256]{1,0:T(8,128)S(1)}, f32[128,256]{1,0:T(8,128)S(1)}, bf16[128,256]{1,0:T(8,128)(2,1)S(1)}, bf16[12...) custom-call(bf16[4096,128]{1,0:T(8,128)(2,1)S(1)} %bitcast.13, bf16[2048,256]{1,0:T(8,128)(2,1)S(1)} %shard_map.95.g_ref, ...), custom_call_target="tpu_custom_call" | custom-call | flops 4026531840 | bytes 2097152 | tf_op jit(solution)/shard_map/pallas_call | solution.py:354
  26.0 0.1 collective-permute-start.3
  26.1 3.0 %collective-permute-start.4 = (bf16[128,256]{1,0:T(8,128)(2,1)S(1)}, bf16[128,256]{1,0:T(8,128)(2,1)S(1)}, u32[]{:S(2)}, u32[]{:S(2)}) collective-permute-start(bf16[128,256]{1,0:T(8,128)(2,1)S(1)} %get-tuple-element.39), channel_id=1, source_target_pairs={{0,2},{1,3},{2,0},{3,1},{4,6},{5,7},{6,4},{7,5},{8,10},{9,11},{10,... | collective-permute-start | bytes 196616 | tf_op jit(solution)/shard_map/ppermute | solution.py:33
  29.1 0.1 collective-permute-start.5
  29.1 2.4 %shard_map.99 = (f32[128,1280]{1,0:T(8,128)S(1)}, f32[512,256]{1,0:T(8,128)S(1)}) custom-call(bf16[4096,128]{1,0:T(8,128)(2,1)S(1)} %bitcast.14, bf16[1280,128]{1,0:T(8,128)(2,1)S(1)} %bitcast.21, bf16[4096,128]{1,0:T(8,128)(2,1)S(1)} %bitcast.18, f32[1,4096]{1,0:T(1,128)S(1)} %reshape.30.lse_ref, bf16[1024,128]{1,0:T(8,128)(2,1)S(1)} %get-tuple-element.33.keys_ref, ...), custom_call_target="tpu_custom_call" | custom-call | flops 838860800 | bytes 2097152 | tf_op jit(solution)/shard_map/pallas_call | solution.py:354
  31.5 1.5 %shard_map.100 = (f32[128,768]{1,0:T(8,128)S(1)}, f32[128,256]{1,0:T(8,128)S(1)}, bf16[128,256]{1,0:T(8,128)(2,1)S(1)}, bf16[128,256]{1,0:T(8,128)(2,1)S(1)}, bf16[128,256]{1,0:T(8,128)(2,1)S(1)}) custom-call(bf16[4096,128]{1,0:T(8,128)(2,1)S(1)} %bitcast.15, bf16[768,128]{1,0:T(8,128)(2,1)S(1)} %bitcast.22, bf16[4096,128]{1,0:T(8,128)(2,1)S(1)} %bitcast.19, ...), custom_call_target="tpu_custom_call" | custom-call | flops 503316480 | bytes 2097152 | tf_op jit(solution)/shard_map/pallas_call | solution.py:354
  33.1 0.1 collective-permute-start.8
  33.2 2.1 %collective-permute-start.9 = (bf16[128,256]{1,0:T(8,128)(2,1)S(1)}, bf16[128,256]{1,0:T(8,128)(2,1)S(1)}, u32[]{:S(2)}, u32[]{:S(2)}) collective-permute-start(bf16[128,256]{1,0:T(8,128)(2,1)S(1)} %get-tuple-element.52), channel_id=1, source_target_pairs={{0,2},{1,3},{2,0},{3,1},{4,6},{5,7},{6,4},{7,5},{8,10},{9,11},{10,... | collective-permute-start | bytes 196616 | tf_op jit(solution)/shard_map/ppermute | solution.py:33
  35.2 0.0 collective-permute-start.10
  35.2 1.2 %shard_map.101 = (bf16[128,256]{1,0:T(8,128)(2,1)S(1)}, bf16[4096,128]{1,0:T(8,128)(2,1)}) custom-call(f32[128,256]{1,0:T(8,128)S(1)} %get-tuple-element.37.refs_0_, bf16[128,256]{1,0:T(8,128)(2,1)S(1)} %collective-permute-done.3.refs_1_, bf16[128,256]{1,0:T(8,128)(2,1)S(1)} %collective-permute-done.4.refs_2_, ...), custom_call_target="tpu_custom_call" | custom-call | tf_op jit(solution)/shard_map/pallas_call | solution.py:284
  36.4 1.2 %collective-permute-done.9.refs_2_ = bf16[128,256]{1,0:T(8,128)(2,1)S(1)} collective-permute-done((bf16[128,256]{1,0:T(8,128)(2,1)S(1)}, bf16[128,256]{1,0:T(8,128)(2,1)S(1)}, u32[]{:S(2)}, u32[]{:S(2)}) %collective-permute-start.9) | collective-permute-done | bytes 65568 | tf_op jit(solution)/shard_map/ppermute | solution.py:33
  37.7 1.9 %collective-permute-done.10.refs_3_ = bf16[128,256]{1,0:T(8,128)(2,1)S(1)} collective-permute-done((bf16[128,256]{1,0:T(8,128)(2,1)S(1)}, bf16[128,256]{1,0:T(8,128)(2,1)S(1)}, u32[]{:S(2)}, u32[]{:S(2)}) %collective-permute-start.10) | collective-permute-done | bytes 65568 | tf_op jit(solution)/shard_map/ppermute | solution.py:33
  39.6 0.7 %shard_map.102 = (bf16[256,128]{1,0:T(8,128)(2,1)}, bf16[256,128]{1,0:T(8,128)(2,1)}) custom-call(f32[128,256]{1,0:T(8,128)S(1)} %get-tuple-element.50.refs_0_, bf16[128,256]{1,0:T(8,128)(2,1)S(1)} %collective-permute-done.8.refs_1_, bf16[128,256]{1,0:T(8,128)(2,1)S(1)} %collective-permute-done.9.refs_2_, ...), custom_call_target="tpu_custom_call" | custom-call | tf_op jit(solution)/shard_map/pallas_call | solution.py:377
  (15 shorter events, 0.1 us)
Async XLA Ops:
  0.6 1.2 %copy-start.2 = (bf16[1,256,16,128]{3,2,1,0:T(8,128)(2,1)S(1)}, bf16[1,256,16,128]{3,2,1,0:T(8,128)(2,1)}, u32[]{:S(2)}) copy-start(bf16[1,256,16,128]{3,2,1,0:T(8,128)(2,1)} %param.11) | copy-start | bytes 3145732
  1.9 16.3 %copy-start = (bf16[1,256,16,128]{3,2,1,0:T(8,128)(2,1)S(1)}, bf16[1,256,16,128]{3,2,1,0:T(8,128)(2,1)}, u32[]{:S(2)}) copy-start(bf16[1,256,16,128]{3,2,1,0:T(8,128)(2,1)} %param.7) | copy-start | bytes 3145732
  2.3 6.9 %copy-start.4 = (bf16[1,256,128]{2,1,0:T(8,128)(2,1)S(1)}, bf16[1,256,128]{2,1,0:T(8,128)(2,1)}, u32[]{:S(2)}) copy-start(bf16[1,256,128]{2,1,0:T(8,128)(2,1)} %param.9) | copy-start | bytes 196612
  2.3 18.4 %collective-permute-start = (bf16[128,16,128]{2,1,0:T(8,128)(2,1)S(1)}, bf16[128,16,128]{2,1,0:T(8,128)(2,1)S(1)}, u32[]{:S(2)}, u32[]{:S(2)}) collective-permute-start(bf16[128,16,128]{2,1,0:T(8,128)(2,1)S(1)} %get-tuple-element.30), channel_id=1, source_target_pairs={{0,28},{4,0},{8,4},{12,8},{16,12},{20,16},{24,20},{28,24},{1,29},{... | collective-permute-start | bytes 1572872 | tf_op jit(solution)/shard_map/ppermute | solution.py:28
  9.2 5.7 %copy-start.5 = (f32[1,16,256]{2,1,0:T(8,128)S(1)}, f32[1,16,256]{2,1,0:T(8,128)}, u32[]{:S(2)}) copy-start(f32[1,16,256]{2,1,0:T(8,128)} %param.12) | copy-start | bytes 49156
  9.2 5.0 %collective-permute-start.1 = (bf16[2,256,128]{2,1,0:T(8,128)(2,1)S(1)}, bf16[2,256,128]{2,1,0:T(8,128)(2,1)S(1)}, u32[]{:S(2)}, u32[]{:S(2)}) collective-permute-start(bf16[2,256,128]{2,1,0:T(8,128)(2,1)S(1)} %constant_dynamic-update-slice_fusion.refs_0_), channel_id=1, source_target_pairs={{0,2},{1,3},{2,0},{3,1},{4,6},{5,7},{6,4},{7,5},{8,10},{9,11},{10,... | collective-permute-start | bytes 393224 | tf_op jit(solution)/shard_map/ppermute | solution.py:33
  14.3 3.9 %collective-permute-start.2 = (bf16[4,256,128]{2,1,0:T(8,128)(2,1)S(1)}, bf16[4,256,128]{2,1,0:T(8,128)(2,1)S(1)}, u32[]{:S(2)}, u32[]{:S(2)}) collective-permute-start(bf16[4,256,128]{2,1,0:T(8,128)(2,1)S(1)} %shard_map.96.refs_0_), channel_id=1, source_target_pairs={{0,1},{1,0},{2,3},{3,2},{4,5},{5,4},{6,7},{7,6},{8,9},{9,8},{10,11... | collective-permute-start | bytes 786440 | tf_op jit(solution)/shard_map/ppermute | solution.py:33
  14.3 14.8 %collective-permute-start.6 = (bf16[80,16,128]{2,1,0:T(8,128)(2,1)S(1)}, bf16[80,16,128]{2,1,0:T(8,128)(2,1)S(1)}, u32[]{:S(2)}, u32[]{:S(2)}) collective-permute-start(bf16[80,16,128]{2,1,0:T(8,128)(2,1)S(1)} %get-tuple-element.42), channel_id=1, source_target_pairs={{0,28},{4,0},{8,4},{12,8},{16,12},{20,16},{24,20},{28,24},{1,29},{... | collective-permute-start | bytes 983048 | tf_op jit(solution)/shard_map/ppermute | solution.py:28
  16.7 1.4 %copy-start.3 = (s32[8]{0:T(128)S(1)}, s32[8]{0:T(128)}, u32[]{:S(2)}) copy-start(s32[8]{0:T(128)} %starts_ref.1) | copy-start | bytes 100
  16.7 14.8 %collective-permute-start.7 = (bf16[48,16,128]{2,1,0:T(8,128)(2,1)S(1)}, bf16[48,16,128]{2,1,0:T(8,128)(2,1)S(1)}, u32[]{:S(2)}, u32[]{:S(2)}) collective-permute-start(bf16[48,16,128]{2,1,0:T(8,128)(2,1)S(1)} %get-tuple-element.46), channel_id=1, source_target_pairs={{0,28},{4,0},{8,4},{12,8},{16,12},{20,16},{24,20},{28,24},{1,29},{... | collective-permute-start | bytes 589832 | tf_op jit(solution)/shard_map/ppermute | solution.py:28
  18.1 2.5 %copy-start.1 = (bf16[1,256,16,128]{3,2,1,0:T(8,128)(2,1)S(1)}, bf16[1,256,16,128]{3,2,1,0:T(8,128)(2,1)}, u32[]{:S(2)}) copy-start(bf16[1,256,16,128]{3,2,1,0:T(8,128)(2,1)} %param.10) | copy-start | bytes 3145732
  26.0 5.5 %collective-permute-start.3 = (bf16[128,256]{1,0:T(8,128)(2,1)S(1)}, bf16[128,256]{1,0:T(8,128)(2,1)S(1)}, u32[]{:S(2)}, u32[]{:S(2)}) collective-permute-start(bf16[128,256]{1,0:T(8,128)(2,1)S(1)} %get-tuple-element.38), channel_id=1, source_target_pairs={{0,1},{1,0},{2,3},{3,2},{4,5},{5,4},{6,7},{7,6},{8,9},{9,8},{10,11... | collective-permute-start | bytes 196616 | tf_op jit(solution)/shard_map/ppermute | solution.py:33
  26.1 9.1 %collective-permute-start.4 = (bf16[128,256]{1,0:T(8,128)(2,1)S(1)}, bf16[128,256]{1,0:T(8,128)(2,1)S(1)}, u32[]{:S(2)}, u32[]{:S(2)}) collective-permute-start(bf16[128,256]{1,0:T(8,128)(2,1)S(1)} %get-tuple-element.39), channel_id=1, source_target_pairs={{0,2},{1,3},{2,0},{3,1},{4,6},{5,7},{6,4},{7,5},{8,10},{9,11},{10,... | collective-permute-start | bytes 196616 | tf_op jit(solution)/shard_map/ppermute | solution.py:33
  29.1 6.2 %collective-permute-start.5 = (bf16[128,256]{1,0:T(8,128)(2,1)S(1)}, bf16[128,256]{1,0:T(8,128)(2,1)S(1)}, u32[]{:S(2)}, u32[]{:S(2)}) collective-permute-start(bf16[128,256]{1,0:T(8,128)(2,1)S(1)} %get-tuple-element.40), channel_id=1, source_target_pairs={{0,3},{1,2},{2,1},{3,0},{4,7},{5,6},{6,5},{7,4},{8,11},{9,10},{10,... | collective-permute-start | bytes 196616 | tf_op jit(solution)/shard_map/ppermute | solution.py:33
  33.1 3.4 %collective-permute-start.8 = (bf16[128,256]{1,0:T(8,128)(2,1)S(1)}, bf16[128,256]{1,0:T(8,128)(2,1)S(1)}, u32[]{:S(2)}, u32[]{:S(2)}) collective-permute-start(bf16[128,256]{1,0:T(8,128)(2,1)S(1)} %get-tuple-element.51), channel_id=1, source_target_pairs={{0,1},{1,0},{2,3},{3,2},{4,5},{5,4},{6,7},{7,6},{8,9},{9,8},{10,11... | collective-permute-start | bytes 196616 | tf_op jit(solution)/shard_map/ppermute | solution.py:33
  33.2 4.5 %collective-permute-start.9 = (bf16[128,256]{1,0:T(8,128)(2,1)S(1)}, bf16[128,256]{1,0:T(8,128)(2,1)S(1)}, u32[]{:S(2)}, u32[]{:S(2)}) collective-permute-start(bf16[128,256]{1,0:T(8,128)(2,1)S(1)} %get-tuple-element.52), channel_id=1, source_target_pairs={{0,2},{1,3},{2,0},{3,1},{4,6},{5,7},{6,4},{7,5},{8,10},{9,11},{10,... | collective-permute-start | bytes 196616 | tf_op jit(solution)/shard_map/ppermute | solution.py:33
  35.2 4.4 %collective-permute-start.10 = (bf16[128,256]{1,0:T(8,128)(2,1)S(1)}, bf16[128,256]{1,0:T(8,128)(2,1)S(1)}, u32[]{:S(2)}, u32[]{:S(2)}) collective-permute-start(bf16[128,256]{1,0:T(8,128)(2,1)S(1)} %get-tuple-element.53), channel_id=1, source_target_pairs={{0,3},{1,2},{2,1},{3,0},{4,7},{5,6},{6,5},{7,4},{8,11},{9,10},{10,... | collective-permute-start | bytes 196616 | tf_op jit(solution)/shard_map/ppermute | solution.py:33

commit v2 on v0

--- a/solution.py
+++ b/solution.py
@@ -10,7 +10,7 @@
 
 KEY_BLOCK = 512
 LANES = 128
-UPPER_CHUNKS = (64, 64)
+UPPER_CHUNKS = (80, 48)
 LOWER_CHUNKS = (80, 48)
 VMEM_LIMIT = 40 * 1024 * 1024
 SORT_FLOPS = 10**9

time: 38.8 us -> 39.2 us (1.010)
  local copies, waits for them, and re-layouts: 2.31 us -> 2.78 us
  Pallas kernels: 12.3 us -> 12.7 us
    unnamed x13, local copies, waits for them, and re-layouts: 2.09 us -> 2.55 us
  transfers between devices with their start and end apart: 12 -> 12, of which waited for: 8 -> 6; matrix products, arithmetic and copies ran while one was open for 3% -> 3% of each run, Pallas kernels for 29% -> 29%
where the time goes in v2:
time: 39.2 us; the launch traced here: 39 us
  starting transfers between devices  14.4 us (37%)
  Pallas kernels  12.7 us (32%)
  waiting for transfers between devices  8.35 us (21%)
  local copies, waits for them, and re-layouts  2.78 us (7%)
  between operations  0.8 us (2%)
    pallas_call x4, Pallas kernels, body(): pl.pallas_call(functools.partial(chunk_kernel, chunk, heads, span_rows, c...  9.18 us
    ppermute x4, starting transfers between devices, from_behind(): lax.ppermute(shard, axis, [(i, (i + by) % length) for i in range(length)])  8.53 us
    ppermute x8, starting transfers between devices, with_partner(): return lax.ppermute(shard, axis, [(i, i ^ step) for i in range(length)])  5.83 us
    ppermute x4, waiting for transfers between devices, from_behind(): lax.ppermute(shard, axis, [(i, (i + by) % length) for i in range(length)])  4.24 us
    ppermute x8, waiting for transfers between devices, with_partner(): return lax.ppermute(shard, axis, [(i, i ^ step) for i in range(length)])  4.11 us
    unnamed x13, local copies, waits for them, and re-layouts  2.55 us
    pallas_call x1, Pallas kernels, finish(): pl.pallas_call(functools.partial(finish_kernel, len(terms), places), out_...  1.16 us
    pallas_call x1, Pallas kernels, sort_keys(): pl.pallas_call(functools.partial(sort_keys_kernel, codes, span_rows, head...  0.79 us
  transfers between devices with their start and end apart: 12, of which 6 were waited for; matrix products, arithmetic and copies ran while one was open for 3% of the time, Pallas kernels for 29%

profile of v2, /device:TPU:0, one launch (start us, length us, event | category | flops | bytes accessed | tf_op | source)
XLA Modules:
  0.0 39.0 jit_solution(11813346047145197360)
XLA Ops:
  0.6 1.2 %copy-done.2 = bf16[1,256,16,128]{3,2,1,0:T(8,128)(2,1)S(1)} copy-done((bf16[1,256,16,128]{3,2,1,0:T(8,128)(2,1)S(1)}, bf16[1,256,16,128]{3,2,1,0:T(8,128)(2,1)}, u32[]{:S(2)}) %copy-start.2) | copy-done | bytes 1048600
  1.9 0.7 %shard_map.94 = (bf16[80,16,128]{2,1,0:T(8,128)(2,1)S(1)}, bf16[48,16,128]{2,1,0:T(8,128)(2,1)S(1)}, bf16[80,16,128]{2,1,0:T(8,128)(2,1)S(1)}, bf16[48,16,128]{2,1,0:T(8,128)(2,1)S(1)}) custom-call(bf16[256,16,128]{2,1,0:T(8,128)(2,1)S(1)} %bitcast.22), custom_call_target="tpu_custom_call" | custom-call | bytes 2097152 | tf_op jit(solution)/shard_map/pallas_call | solution.py:52
  2.6 6.0 %collective-permute-start.3 = (bf16[80,16,128]{2,1,0:T(8,128)(2,1)S(1)}, bf16[80,16,128]{2,1,0:T(8,128)(2,1)S(1)}, u32[]{:S(2)}, u32[]{:S(2)}) collective-permute-start(bf16[80,16,128]{2,1,0:T(8,128)(2,1)S(1)} %get-tuple-element.34), channel_id=1, source_target_pairs={{0,28},{4,0},{8,4},{12,8},{16,12},{20,16},{24,20},{28,24},{1,29},{... | collective-permute-start | bytes 983048 | tf_op jit(solution)/shard_map/ppermute | solution.py:27
  8.7 0.8 %constant_dynamic-update-slice_fusion.1 = bf16[2,256,128]{2,1,0:T(8,128)(2,1)S(1)} fusion(bf16[1,256,128]{2,1,0:T(8,128)(2,1)} %param.8), kind=kLoop, calls=%fused_computation.1 | loop fusion | bytes 131072
  9.5 1.6 %collective-permute-start.1 = (bf16[2,256,128]{2,1,0:T(8,128)(2,1)S(1)}, bf16[2,256,128]{2,1,0:T(8,128)(2,1)S(1)}, u32[]{:S(2)}, u32[]{:S(2)}) collective-permute-start(bf16[2,256,128]{2,1,0:T(8,128)(2,1)S(1)} %constant_dynamic-update-slice_fusion.refs_0_), channel_id=1, source_target_pairs={{0,2},{1,3},{2,0},{3,1},{4,6},{5,7},{6,4},{7,5},{8,10},{9,11},{10,... | collective-permute-start | bytes 393224 | tf_op jit(solution)/shard_map/ppermute | solution.py:32
  11.1 0.5 %collective-permute-start = (bf16[48,16,128]{2,1,0:T(8,128)(2,1)S(1)}, bf16[48,16,128]{2,1,0:T(8,128)(2,1)S(1)}, u32[]{:S(2)}, u32[]{:S(2)}) collective-permute-start(bf16[48,16,128]{2,1,0:T(8,128)(2,1)S(1)} %get-tuple-element.33), channel_id=1, source_target_pairs={{0,28},{4,0},{8,4},{12,8},{16,12},{20,16},{24,20},{28,24},{1,29},{... | collective-permute-start | bytes 589832 | tf_op jit(solution)/shard_map/ppermute | solution.py:27
  11.7 1.4 %collective-permute-start.7 = (bf16[80,16,128]{2,1,0:T(8,128)(2,1)S(1)}, bf16[80,16,128]{2,1,0:T(8,128)(2,1)S(1)}, u32[]{:S(2)}, u32[]{:S(2)}) collective-permute-start(bf16[80,16,128]{2,1,0:T(8,128)(2,1)S(1)} %get-tuple-element.48), channel_id=1, source_target_pairs={{0,28},{4,0},{8,4},{12,8},{16,12},{20,16},{24,20},{28,24},{1,29},{... | collective-permute-start | bytes 983048 | tf_op jit(solution)/shard_map/ppermute | solution.py:27
  13.0 0.1 copy.11
  13.1 0.1 reshape.33.lse_ref
  13.2 1.3 %collective-permute-done.1.refs_1_ = bf16[2,256,128]{2,1,0:T(8,128)(2,1)S(1)} collective-permute-done((bf16[2,256,128]{2,1,0:T(8,128)(2,1)S(1)}, bf16[2,256,128]{2,1,0:T(8,128)(2,1)S(1)}, u32[]{:S(2)}, u32[]{:S(2)}) %collective-permute-start.1) | collective-permute-done | bytes 131104 | tf_op jit(solution)/shard_map/ppermute | solution.py:32
  14.6 0.1 collective-permute-start.2
  14.7 0.6 %collective-permute-start.8 = (bf16[48,16,128]{2,1,0:T(8,128)(2,1)S(1)}, bf16[48,16,128]{2,1,0:T(8,128)(2,1)S(1)}, u32[]{:S(2)}, u32[]{:S(2)}) collective-permute-start(bf16[48,16,128]{2,1,0:T(8,128)(2,1)S(1)} %get-tuple-element.52), channel_id=1, source_target_pairs={{0,28},{4,0},{8,4},{12,8},{16,12},{20,16},{24,20},{28,24},{1,29},{... | collective-permute-start | bytes 589832 | tf_op jit(solution)/shard_map/ppermute | solution.py:27
  15.2 1.5 %collective-permute-done.3 = bf16[80,16,128]{2,1,0:T(8,128)(2,1)S(1)} collective-permute-done((bf16[80,16,128]{2,1,0:T(8,128)(2,1)S(1)}, bf16[80,16,128]{2,1,0:T(8,128)(2,1)S(1)}, u32[]{:S(2)}, u32[]{:S(2)}) %collective-permute-start.3) | collective-permute-done | bytes 327712 | tf_op jit(solution)/shard_map/ppermute | solution.py:27
  16.8 0.2 shard_map.97.g_ref
  17.0 0.5 %copy-done.3 = s32[8]{0:T(128)S(1)} copy-done((s32[8]{0:T(128)S(1)}, s32[8]{0:T(128)}, u32[]{:S(2)}) %copy-start.3) | copy-done | bytes 56
  17.4 0.8 %shard_map.96 = (bf16[1024,128]{1,0:T(8,128)(2,1)S(1)}, bf16[1024,256]{1,0:T(8,128)(2,1)S(1)}, bf16[128,1024]{1,0:T(8,128)(2,1)S(1)}, f32[8,128]{1,0:T(8,128)S(1)}) custom-call(s32[8]{0:T(128)S(1)} %copy-done.3, bf16[4,256,128]{2,1,0:T(8,128)(2,1)S(1)} %shard_map.95.refs_0_, bf16[4,256,128]{2,1,0:T(8,128)(2,1)S(1)} %collective-permute-done.2.refs_1_), custom_call_target="tpu_custom_call" | custom-call | flops 1000000000 | bytes 1048576 | tf_op jit(solution)/shard_map/pallas_call | solution.py:145
  18.2 3.9 %shard_map.98 = (f32[128,1280]{1,0:T(8,128)S(1)}, f32[1024,256]{1,0:T(8,128)S(1)}) custom-call(bf16[4096,128]{1,0:T(8,128)(2,1)S(1)} %bitcast.13, bf16[1280,256]{1,0:T(8,128)(2,1)S(1)} %shard_map.97.g_ref, bf16[4096,128]{1,0:T(8,128)(2,1)S(1)} %bitcast.18, f32[1,4096]{1,0:T(1,128)S(1)} %reshape.33.lse_ref, bf16[1024,128]{1,0:T(8,128)(2,1)S(1)} %get-tuple-element.37.keys_ref, ...), custom_call_target="tpu_custom_call" | custom-call | flops 2516582400 | bytes 2097152 | tf_op jit(solution)/shard_map/pallas_call | solution.py:349
  22.2 2.7 %shard_map.99 = (f32[128,768]{1,0:T(8,128)S(1)}, f32[1024,256]{1,0:T(8,128)S(1)}, f32[128,256]{1,0:T(8,128)S(1)}, bf16[128,256]{1,0:T(8,128)(2,1)S(1)}, bf16[128...) custom-call(bf16[4096,128]{1,0:T(8,128)(2,1)S(1)} %bitcast.14, bf16[768,128]{1,0:T(8,128)(2,1)S(1)} %bitcast.26, ...), custom_call_target="tpu_custom_call" | custom-call | flops 1509949440 | bytes 2097152 | tf_op jit(solution)/shard_map/pallas_call | solution.py:349
  24.9 0.1 collective-permute-start.4
  25.0 0.4 %collective-permute-start.5 = (bf16[128,256]{1,0:T(8,128)(2,1)S(1)}, bf16[128,256]{1,0:T(8,128)(2,1)S(1)}, u32[]{:S(2)}, u32[]{:S(2)}) collective-permute-start(bf16[128,256]{1,0:T(8,128)(2,1)S(1)} %get-tuple-element.44), channel_id=1, source_target_pairs={{0,2},{1,3},{2,0},{3,1},{4,6},{5,7},{6,4},{7,5},{8,10},{9,11},{10,... | collective-permute-start | bytes 196616 | tf_op jit(solution)/shard_map/ppermute | solution.py:32
  25.4 1.4 %collective-permute-start.6 = (bf16[128,256]{1,0:T(8,128)(2,1)S(1)}, bf16[128,256]{1,0:T(8,128)(2,1)S(1)}, u32[]{:S(2)}, u32[]{:S(2)}) collective-permute-start(bf16[128,256]{1,0:T(8,128)(2,1)S(1)} %get-tuple-element.45), channel_id=1, source_target_pairs={{0,3},{1,2},{2,1},{3,0},{4,7},{5,6},{6,5},{7,4},{8,11},{9,10},{10,... | collective-permute-start | bytes 196616 | tf_op jit(solution)/shard_map/ppermute | solution.py:32
  26.8 1.2 %collective-permute-done.7 = bf16[80,16,128]{2,1,0:T(8,128)(2,1)S(1)} collective-permute-done((bf16[80,16,128]{2,1,0:T(8,128)(2,1)S(1)}, bf16[80,16,128]{2,1,0:T(8,128)(2,1)S(1)}, u32[]{:S(2)}, u32[]{:S(2)}) %collective-permute-start.7) | collective-permute-done | bytes 327712 | tf_op jit(solution)/shard_map/ppermute | solution.py:27
  28.0 1.5 %shard_map.100 = (f32[128,1280]{1,0:T(8,128)S(1)}, f32[512,256]{1,0:T(8,128)S(1)}) custom-call(bf16[4096,128]{1,0:T(8,128)(2,1)S(1)} %bitcast.15, bf16[1280,128]{1,0:T(8,128)(2,1)S(1)} %bitcast.23, bf16[4096,128]{1,0:T(8,128)(2,1)S(1)} %bitcast.20, f32[1,4096]{1,0:T(1,128)S(1)} %reshape.33.lse_ref, bf16[1024,128]{1,0:T(8,128)(2,1)S(1)} %get-tuple-element.37.keys_ref, ...), custom_call_target="tpu_custom_call" | custom-call | flops 838860800 | bytes 2097152 | tf_op jit(solution)/shard_map/pallas_call | solution.py:349
  29.5 1.6 %collective-permute-done.8 = bf16[48,16,128]{2,1,0:T(8,128)(2,1)S(1)} collective-permute-done((bf16[48,16,128]{2,1,0:T(8,128)(2,1)S(1)}, bf16[48,16,128]{2,1,0:T(8,128)(2,1)S(1)}, u32[]{:S(2)}, u32[]{:S(2)}) %collective-permute-start.8) | collective-permute-done | bytes 196640 | tf_op jit(solution)/shard_map/ppermute | solution.py:27
  31.1 1.0 %shard_map.101 = (f32[128,768]{1,0:T(8,128)S(1)}, f32[128,256]{1,0:T(8,128)S(1)}, bf16[128,256]{1,0:T(8,128)(2,1)S(1)}, bf16[128,256]{1,0:T(8,128)(2,1)S(1)}, bf16[128,256]{1,0:T(8,128)(2,1)S(1)}) custom-call(bf16[4096,128]{1,0:T(8,128)(2,1)S(1)} %bitcast.16, bf16[768,128]{1,0:T(8,128)(2,1)S(1)} %bitcast.24, bf16[4096,128]{1,0:T(8,128)(2,1)S(1)} %bitcast.21, ...), custom_call_target="tpu_custom_call" | custom-call | flops 503316480 | bytes 2097152 | tf_op jit(solution)/shard_map/pallas_call | solution.py:349
  32.1 0.1 collective-permute-start.9
  32.2 2.1 %collective-permute-start.10 = (bf16[128,256]{1,0:T(8,128)(2,1)S(1)}, bf16[128,256]{1,0:T(8,128)(2,1)S(1)}, u32[]{:S(2)}, u32[]{:S(2)}) collective-permute-start(bf16[128,256]{1,0:T(8,128)(2,1)S(1)} %get-tuple-element.58), channel_id=1, source_target_pairs={{0,2},{1,3},{2,0},{3,1},{4,6},{5,7},{6,4},{7,5},{8,10},{9,11},{10,... | collective-permute-start | bytes 196616 | tf_op jit(solution)/shard_map/ppermute | solution.py:32
  34.3 0.1 collective-permute-start.11
  34.4 1.2 %shard_map.102 = (bf16[128,256]{1,0:T(8,128)(2,1)S(1)}, bf16[4096,128]{1,0:T(8,128)(2,1)}) custom-call(f32[128,256]{1,0:T(8,128)S(1)} %get-tuple-element.42.refs_0_, bf16[128,256]{1,0:T(8,128)(2,1)S(1)} %collective-permute-done.4.refs_1_, bf16[128,256]{1,0:T(8,128)(2,1)S(1)} %collective-permute-done.5.refs_2_, ...), custom_call_target="tpu_custom_call" | custom-call | tf_op jit(solution)/shard_map/pallas_call | solution.py:279
  35.6 1.4 %collective-permute-done.10.refs_2_ = bf16[128,256]{1,0:T(8,128)(2,1)S(1)} collective-permute-done((bf16[128,256]{1,0:T(8,128)(2,1)S(1)}, bf16[128,256]{1,0:T(8,128)(2,1)S(1)}, u32[]{:S(2)}, u32[]{:S(2)}) %collective-permute-start.10) | collective-permute-done | bytes 65568 | tf_op jit(solution)/shard_map/ppermute | solution.py:32
  37.0 1.4 %collective-permute-done.11.refs_3_ = bf16[128,256]{1,0:T(8,128)(2,1)S(1)} collective-permute-done((bf16[128,256]{1,0:T(8,128)(2,1)S(1)}, bf16[128,256]{1,0:T(8,128)(2,1)S(1)}, u32[]{:S(2)}, u32[]{:S(2)}) %collective-permute-start.11) | collective-permute-done | bytes 65568 | tf_op jit(solution)/shard_map/ppermute | solution.py:32
  38.4 0.7 %shard_map.103 = (bf16[256,128]{1,0:T(8,128)(2,1)}, bf16[256,128]{1,0:T(8,128)(2,1)}) custom-call(f32[128,256]{1,0:T(8,128)S(1)} %get-tuple-element.56.refs_0_, bf16[128,256]{1,0:T(8,128)(2,1)S(1)} %collective-permute-done.9.refs_1_, bf16[128,256]{1,0:T(8,128)(2,1)S(1)} %collective-permute-done.10.refs_2_, ...), custom_call_target="tpu_custom_call" | custom-call | tf_op jit(solution)/shard_map/pallas_call | solution.py:372
  (18 shorter events, 0.1 us)
Async XLA Ops:
  0.6 1.2 %copy-start.2 = (bf16[1,256,16,128]{3,2,1,0:T(8,128)(2,1)S(1)}, bf16[1,256,16,128]{3,2,1,0:T(8,128)(2,1)}, u32[]{:S(2)}) copy-start(bf16[1,256,16,128]{3,2,1,0:T(8,128)(2,1)} %param.11) | copy-start | bytes 3145732
  1.9 14.9 %copy-start.1 = (bf16[1,256,16,128]{3,2,1,0:T(8,128)(2,1)S(1)}, bf16[1,256,16,128]{3,2,1,0:T(8,128)(2,1)}, u32[]{:S(2)}) copy-start(bf16[1,256,16,128]{3,2,1,0:T(8,128)(2,1)} %param.10) | copy-start | bytes 3145732
  2.6 6.9 %copy-start.4 = (bf16[1,256,128]{2,1,0:T(8,128)(2,1)S(1)}, bf16[1,256,128]{2,1,0:T(8,128)(2,1)}, u32[]{:S(2)}) copy-start(bf16[1,256,128]{2,1,0:T(8,128)(2,1)} %param.9) | copy-start | bytes 196612
  2.6 14.1 %collective-permute-start.3 = (bf16[80,16,128]{2,1,0:T(8,128)(2,1)S(1)}, bf16[80,16,128]{2,1,0:T(8,128)(2,1)S(1)}, u32[]{:S(2)}, u32[]{:S(2)}) collective-permute-start(bf16[80,16,128]{2,1,0:T(8,128)(2,1)S(1)} %get-tuple-element.34), channel_id=1, source_target_pairs={{0,28},{4,0},{8,4},{12,8},{16,12},{20,16},{24,20},{28,24},{1,29},{... | collective-permute-start | bytes 983048 | tf_op jit(solution)/shard_map/ppermute | solution.py:27
  9.5 3.5 %copy-start.5 = (f32[1,16,256]{2,1,0:T(8,128)S(1)}, f32[1,16,256]{2,1,0:T(8,128)}, u32[]{:S(2)}) copy-start(f32[1,16,256]{2,1,0:T(8,128)} %param.12) | copy-start | bytes 49156
  9.5 5.0 %collective-permute-start.1 = (bf16[2,256,128]{2,1,0:T(8,128)(2,1)S(1)}, bf16[2,256,128]{2,1,0:T(8,128)(2,1)S(1)}, u32[]{:S(2)}, u32[]{:S(2)}) collective-permute-start(bf16[2,256,128]{2,1,0:T(8,128)(2,1)S(1)} %constant_dynamic-update-slice_fusion.refs_0_), channel_id=1, source_target_pairs={{0,2},{1,3},{2,0},{3,1},{4,6},{5,7},{6,4},{7,5},{8,10},{9,11},{10,... | collective-permute-start | bytes 393224 | tf_op jit(solution)/shard_map/ppermute | solution.py:32
  11.1 11.1 %collective-permute-start = (bf16[48,16,128]{2,1,0:T(8,128)(2,1)S(1)}, bf16[48,16,128]{2,1,0:T(8,128)(2,1)S(1)}, u32[]{:S(2)}, u32[]{:S(2)}) collective-permute-start(bf16[48,16,128]{2,1,0:T(8,128)(2,1)S(1)} %get-tuple-element.33), channel_id=1, source_target_pairs={{0,28},{4,0},{8,4},{12,8},{16,12},{20,16},{24,20},{28,24},{1,29},{... | collective-permute-start | bytes 589832 | tf_op jit(solution)/shard_map/ppermute | solution.py:27
  11.7 16.3 %collective-permute-start.7 = (bf16[80,16,128]{2,1,0:T(8,128)(2,1)S(1)}, bf16[80,16,128]{2,1,0:T(8,128)(2,1)S(1)}, u32[]{:S(2)}, u32[]{:S(2)}) collective-permute-start(bf16[80,16,128]{2,1,0:T(8,128)(2,1)S(1)} %get-tuple-element.48), channel_id=1, source_target_pairs={{0,28},{4,0},{8,4},{12,8},{16,12},{20,16},{24,20},{28,24},{1,29},{... | collective-permute-start | bytes 983048 | tf_op jit(solution)/shard_map/ppermute | solution.py:27
  14.6 2.4 %collective-permute-start.2 = (bf16[4,256,128]{2,1,0:T(8,128)(2,1)S(1)}, bf16[4,256,128]{2,1,0:T(8,128)(2,1)S(1)}, u32[]{:S(2)}, u32[]{:S(2)}) collective-permute-start(bf16[4,256,128]{2,1,0:T(8,128)(2,1)S(1)} %shard_map.95.refs_0_), channel_id=1, source_target_pairs={{0,1},{1,0},{2,3},{3,2},{4,5},{5,4},{6,7},{7,6},{8,9},{9,8},{10,11... | collective-permute-start | bytes 786440 | tf_op jit(solution)/shard_map/ppermute | solution.py:32
  14.7 16.4 %collective-permute-start.8 = (bf16[48,16,128]{2,1,0:T(8,128)(2,1)S(1)}, bf16[48,16,128]{2,1,0:T(8,128)(2,1)S(1)}, u32[]{:S(2)}, u32[]{:S(2)}) collective-permute-start(bf16[48,16,128]{2,1,0:T(8,128)(2,1)S(1)} %get-tuple-element.52), channel_id=1, source_target_pairs={{0,28},{4,0},{8,4},{12,8},{16,12},{20,16},{24,20},{28,24},{1,29},{... | collective-permute-start | bytes 589832 | tf_op jit(solution)/shard_map/ppermute | solution.py:27
  16.8 0.7 %copy-start.3 = (s32[8]{0:T(128)S(1)}, s32[8]{0:T(128)}, u32[]{:S(2)}) copy-start(s32[8]{0:T(128)} %starts_ref.1) | copy-start | bytes 100
  16.9 1.3 %copy-start = (bf16[1,256,16,128]{3,2,1,0:T(8,128)(2,1)S(1)}, bf16[1,256,16,128]{3,2,1,0:T(8,128)(2,1)}, u32[]{:S(2)}) copy-start(bf16[1,256,16,128]{3,2,1,0:T(8,128)(2,1)} %param.7) | copy-start | bytes 3145732
  24.9 6.2 %collective-permute-start.4 = (bf16[128,256]{1,0:T(8,128)(2,1)S(1)}, bf16[128,256]{1,0:T(8,128)(2,1)S(1)}, u32[]{:S(2)}, u32[]{:S(2)}) collective-permute-start(bf16[128,256]{1,0:T(8,128)(2,1)S(1)} %get-tuple-element.43), channel_id=1, source_target_pairs={{0,1},{1,0},{2,3},{3,2},{4,5},{5,4},{6,7},{7,6},{8,9},{9,8},{10,11... | collective-permute-start | bytes 196616 | tf_op jit(solution)/shard_map/ppermute | solution.py:32
  25.0 9.4 %collective-permute-start.5 = (bf16[128,256]{1,0:T(8,128)(2,1)S(1)}, bf16[128,256]{1,0:T(8,128)(2,1)S(1)}, u32[]{:S(2)}, u32[]{:S(2)}) collective-permute-start(bf16[128,256]{1,0:T(8,128)(2,1)S(1)} %get-tuple-element.44), channel_id=1, source_target_pairs={{0,2},{1,3},{2,0},{3,1},{4,6},{5,7},{6,4},{7,5},{8,10},{9,11},{10,... | collective-permute-start | bytes 196616 | tf_op jit(solution)/shard_map/ppermute | solution.py:32
  25.4 9.0 %collective-permute-start.6 = (bf16[128,256]{1,0:T(8,128)(2,1)S(1)}, bf16[128,256]{1,0:T(8,128)(2,1)S(1)}, u32[]{:S(2)}, u32[]{:S(2)}) collective-permute-start(bf16[128,256]{1,0:T(8,128)(2,1)S(1)} %get-tuple-element.45), channel_id=1, source_target_pairs={{0,3},{1,2},{2,1},{3,0},{4,7},{5,6},{6,5},{7,4},{8,11},{9,10},{10,... | collective-permute-start | bytes 196616 | tf_op jit(solution)/shard_map/ppermute | solution.py:32
  32.1 3.4 %collective-permute-start.9 = (bf16[128,256]{1,0:T(8,128)(2,1)S(1)}, bf16[128,256]{1,0:T(8,128)(2,1)S(1)}, u32[]{:S(2)}, u32[]{:S(2)}) collective-permute-start(bf16[128,256]{1,0:T(8,128)(2,1)S(1)} %get-tuple-element.57), channel_id=1, source_target_pairs={{0,1},{1,0},{2,3},{3,2},{4,5},{5,4},{6,7},{7,6},{8,9},{9,8},{10,11... | collective-permute-start | bytes 196616 | tf_op jit(solution)/shard_map/ppermute | solution.py:32
  32.2 4.8 %collective-permute-start.10 = (bf16[128,256]{1,0:T(8,128)(2,1)S(1)}, bf16[128,256]{1,0:T(8,128)(2,1)S(1)}, u32[]{:S(2)}, u32[]{:S(2)}) collective-permute-start(bf16[128,256]{1,0:T(8,128)(2,1)S(1)} %get-tuple-element.58), channel_id=1, source_target_pairs={{0,2},{1,3},{2,0},{3,1},{4,6},{5,7},{6,4},{7,5},{8,10},{9,11},{10,... | collective-permute-start | bytes 196616 | tf_op jit(solution)/shard_map/ppermute | solution.py:32
  34.3 4.0 %collective-permute-start.11 = (bf16[128,256]{1,0:T(8,128)(2,1)S(1)}, bf16[128,256]{1,0:T(8,128)(2,1)S(1)}, u32[]{:S(2)}, u32[]{:S(2)}) collective-permute-start(bf16[128,256]{1,0:T(8,128)(2,1)S(1)} %get-tuple-element.59), channel_id=1, source_target_pairs={{0,3},{1,2},{2,1},{3,0},{4,7},{5,6},{6,5},{7,4},{8,11},{9,10},{10,... | collective-permute-start | bytes 196616 | tf_op jit(solution)/shard_map/ppermute | solution.py:32

commit v3 on v0

--- a/solution.py
+++ b/solution.py
@@ -36,16 +36,9 @@
     return pltpu.CompilerParams(vmem_limit_bytes=limit)
 
 
-def cut_kernel(cuts, source_ref, *refs):
-    *out_refs, sems = refs
-    copies = [
-        pltpu.make_async_copy(source_ref.at[pl.ds(first, size)], out_ref, sems.at[i])
-        for i, ((first, size), out_ref) in enumerate(zip(cuts, out_refs))
-    ]
-    for copy in copies:
-        copy.start()
-    for copy in copies:
-        copy.wait()
+def cut_kernel(cuts, source_ref, *out_refs):
+    for (first, size), out_ref in zip(cuts, out_refs):
+        out_ref[...] = source_ref[first : first + size]
 
 
 def cut(source, cuts):
@@ -54,9 +47,8 @@
         out_shape=[
             jax.ShapeDtypeStruct((size, *source.shape[1:]), source.dtype) for _, size in cuts
         ],
-        in_specs=[ANYWHERE],
-        out_specs=[ANYWHERE] * len(cuts),
-        scratch_shapes=[pltpu.SemaphoreType.DMA((len(cuts),))],
+        in_specs=[WHOLE],
+        out_specs=[WHOLE] * len(cuts),
         compiler_params=params(),
         cost_estimate=pl.CostEstimate(
             flops=0, bytes_accessed=2 * source.size * source.dtype.itemsize, transcendentals=0

time: 38.8 us -> 38.3 us (0.987)
  starting transfers between devices: 14.5 us -> 14 us
  Pallas kernels: 12.3 us -> 11.9 us
    ppermute x8, starting transfers between devices: 5.97 us -> 5.52 us  [with_partner(): return lax.ppermute(shard, axis, [(i, i ^ step) for i in range(length)])]
  transfers between devices with their start and end apart: 12 -> 12, of which waited for: 8 -> 8; matrix products, arithmetic and copies ran while one was open for 3% -> 3% of each run, Pallas kernels for 29% -> 30%
where the time goes in v3:
time: 38.3 us; the launch traced here: 37.8 us
  starting transfers between devices  14 us (37%)
  Pallas kernels  11.9 us (31%)
  waiting for transfers between devices  8.79 us (23%)
  local copies, waits for them, and re-layouts  2.31 us (6%)
  between operations  0.78 us (2%)
    pallas_call x4, Pallas kernels, body(): pl.pallas_call(functools.partial(chunk_kernel, chunk, heads, span_rows, c...  9.09 us
    ppermute x4, starting transfers between devices, from_behind(): lax.ppermute(shard, axis, [(i, (i + by) % length) for i in range(length)])  8.53 us
    ppermute x8, starting transfers between devices, with_partner(): return lax.ppermute(shard, axis, [(i, i ^ step) for i in range(length)])  5.52 us
    ppermute x8, waiting for transfers between devices, with_partner(): return lax.ppermute(shard, axis, [(i, i ^ step) for i in range(length)])  4.61 us
    ppermute x4, waiting for transfers between devices, from_behind(): lax.ppermute(shard, axis, [(i, (i + by) % length) for i in range(length)])  4.18 us
    unnamed x13, local copies, waits for them, and re-layouts  2.09 us
    pallas_call x1, Pallas kernels, finish(): pl.pallas_call(functools.partial(finish_kernel, len(terms), places), out_...  1.13 us
    pallas_call x1, Pallas kernels, sort_keys(): pl.pallas_call(functools.partial(sort_keys_kernel, codes, span_rows, head...  0.79 us
  transfers between devices with their start and end apart: 12, of which 8 were waited for; matrix products, arithmetic and copies ran while one was open for 3% of the time, Pallas kernels for 30%

profile of v3, /device:TPU:0, one launch (start us, length us, event | category | flops | bytes accessed | tf_op | source)
XLA Modules:
  0.0 37.8 jit_solution(13339480590607464614)
XLA Ops:
  0.6 1.2 %copy-done.2 = bf16[1,256,16,128]{3,2,1,0:T(8,128)(2,1)S(1)} copy-done((bf16[1,256,16,128]{3,2,1,0:T(8,128)(2,1)S(1)}, bf16[1,256,16,128]{3,2,1,0:T(8,128)(2,1)}, u32[]{:S(2)}) %copy-start.2) | copy-done | bytes 1048600
  1.9 6.0 %collective-permute-start.3 = (bf16[64,16,128]{2,1,0:T(8,128)(2,1)S(1)}, bf16[64,16,128]{2,1,0:T(8,128)(2,1)S(1)}, u32[]{:S(2)}, u32[]{:S(2)}) collective-permute-start(bf16[64,16,128]{2,1,0:T(8,128)(2,1)S(1)} %get-tuple-element.34), channel_id=1, source_target_pairs={{0,28},{4,0},{8,4},{12,8},{16,12},{20,16},{24,20},{28,24},{1,29},{... | collective-permute-start | bytes 786440 | tf_op jit(solution)/shard_map/ppermute | solution.py:27
  8.0 0.8 %constant_dynamic-update-slice_fusion.1 = bf16[2,256,128]{2,1,0:T(8,128)(2,1)S(1)} fusion(bf16[1,256,128]{2,1,0:T(8,128)(2,1)} %param.8), kind=kLoop, calls=%fused_computation.1 | loop fusion | bytes 131072
  8.8 1.6 %collective-permute-start.1 = (bf16[2,256,128]{2,1,0:T(8,128)(2,1)S(1)}, bf16[2,256,128]{2,1,0:T(8,128)(2,1)S(1)}, u32[]{:S(2)}, u32[]{:S(2)}) collective-permute-start(bf16[2,256,128]{2,1,0:T(8,128)(2,1)S(1)} %constant_dynamic-update-slice_fusion.refs_0_), channel_id=1, source_target_pairs={{0,2},{1,3},{2,0},{3,1},{4,6},{5,7},{6,4},{7,5},{8,10},{9,11},{10,... | collective-permute-start | bytes 393224 | tf_op jit(solution)/shard_map/ppermute | solution.py:32
  10.4 0.5 %collective-permute-start = (bf16[64,16,128]{2,1,0:T(8,128)(2,1)S(1)}, bf16[64,16,128]{2,1,0:T(8,128)(2,1)S(1)}, u32[]{:S(2)}, u32[]{:S(2)}) collective-permute-start(bf16[64,16,128]{2,1,0:T(8,128)(2,1)S(1)} %get-tuple-element.33), channel_id=1, source_target_pairs={{0,28},{4,0},{8,4},{12,8},{16,12},{20,16},{24,20},{28,24},{1,29},{... | collective-permute-start | bytes 786440 | tf_op jit(solution)/shard_map/ppermute | solution.py:27
  11.0 1.4 %collective-permute-start.7 = (bf16[80,16,128]{2,1,0:T(8,128)(2,1)S(1)}, bf16[80,16,128]{2,1,0:T(8,128)(2,1)S(1)}, u32[]{:S(2)}, u32[]{:S(2)}) collective-permute-start(bf16[80,16,128]{2,1,0:T(8,128)(2,1)S(1)} %get-tuple-element.48), channel_id=1, source_target_pairs={{0,28},{4,0},{8,4},{12,8},{16,12},{20,16},{24,20},{28,24},{1,29},{... | collective-permute-start | bytes 983048 | tf_op jit(solution)/shard_map/ppermute | solution.py:27
  12.3 0.1 copy.11
  12.4 0.1 reshape.33.lse_ref
  12.6 1.3 %collective-permute-done.1.refs_1_ = bf16[2,256,128]{2,1,0:T(8,128)(2,1)S(1)} collective-permute-done((bf16[2,256,128]{2,1,0:T(8,128)(2,1)S(1)}, bf16[2,256,128]{2,1,0:T(8,128)(2,1)S(1)}, u32[]{:S(2)}, u32[]{:S(2)}) %collective-permute-start.1) | collective-permute-done | bytes 131104 | tf_op jit(solution)/shard_map/ppermute | solution.py:32
  13.9 0.1 collective-permute-start.2
  14.0 0.6 %collective-permute-start.8 = (bf16[48,16,128]{2,1,0:T(8,128)(2,1)S(1)}, bf16[48,16,128]{2,1,0:T(8,128)(2,1)S(1)}, u32[]{:S(2)}, u32[]{:S(2)}) collective-permute-start(bf16[48,16,128]{2,1,0:T(8,128)(2,1)S(1)} %get-tuple-element.52), channel_id=1, source_target_pairs={{0,28},{4,0},{8,4},{12,8},{16,12},{20,16},{24,20},{28,24},{1,29},{... | collective-permute-start | bytes 589832 | tf_op jit(solution)/shard_map/ppermute | solution.py:27
  14.6 0.1 collective-permute-done.3
  14.7 0.1 shard_map.97.g_ref
  14.8 0.7 %collective-permute-done.2.refs_1_ = bf16[4,256,128]{2,1,0:T(8,128)(2,1)S(1)} collective-permute-done((bf16[4,256,128]{2,1,0:T(8,128)(2,1)S(1)}, bf16[4,256,128]{2,1,0:T(8,128)(2,1)S(1)}, u32[]{:S(2)}, u32[]{:S(2)}) %collective-permute-start.2) | collective-permute-done | bytes 262176 | tf_op jit(solution)/shard_map/ppermute | solution.py:32
  15.5 0.8 %shard_map.96 = (bf16[1024,128]{1,0:T(8,128)(2,1)S(1)}, bf16[1024,256]{1,0:T(8,128)(2,1)S(1)}, bf16[128,1024]{1,0:T(8,128)(2,1)S(1)}, f32[8,128]{1,0:T(8,128)S(1)}) custom-call(s32[8]{0:T(128)S(1)} %copy-done.3, bf16[4,256,128]{2,1,0:T(8,128)(2,1)S(1)} %shard_map.95.refs_0_, bf16[4,256,128]{2,1,0:T(8,128)(2,1)S(1)} %collective-permute-done.2.refs_1_), custom_call_target="tpu_custom_call" | custom-call | flops 1000000000 | bytes 1048576 | tf_op jit(solution)/shard_map/pallas_call | solution.py:137
  16.3 3.2 %shard_map.98 = (f32[128,1024]{1,0:T(8,128)S(1)}, f32[1024,256]{1,0:T(8,128)S(1)}) custom-call(bf16[4096,128]{1,0:T(8,128)(2,1)S(1)} %bitcast.13, bf16[1024,256]{1,0:T(8,128)(2,1)S(1)} %shard_map.97.g_ref, bf16[4096,128]{1,0:T(8,128)(2,1)S(1)} %bitcast.18, f32[1,4096]{1,0:T(1,128)S(1)} %reshape.33.lse_ref, bf16[1024,128]{1,0:T(8,128)(2,1)S(1)} %get-tuple-element.37.keys_ref, ...), custom_call_target="tpu_custom_call" | custom-call | flops 2013265920 | bytes 2097152 | tf_op jit(solution)/shard_map/pallas_call | solution.py:341
  19.5 0.8 %collective-permute-done = bf16[64,16,128]{2,1,0:T(8,128)(2,1)S(1)} collective-permute-done((bf16[64,16,128]{2,1,0:T(8,128)(2,1)S(1)}, bf16[64,16,128]{2,1,0:T(8,128)(2,1)S(1)}, u32[]{:S(2)}, u32[]{:S(2)}) %collective-permute-start) | collective-permute-done | bytes 262176 | tf_op jit(solution)/shard_map/ppermute | solution.py:27
  20.3 3.4 %shard_map.99 = (f32[128,1024]{1,0:T(8,128)S(1)}, f32[1024,256]{1,0:T(8,128)S(1)}, f32[128,256]{1,0:T(8,128)S(1)}, bf16[128,256]{1,0:T(8,128)(2,1)S(1)}, bf16[12...) custom-call(bf16[4096,128]{1,0:T(8,128)(2,1)S(1)} %bitcast.14, bf16[1024,128]{1,0:T(8,128)(2,1)S(1)} %bitcast.25, ...), custom_call_target="tpu_custom_call" | custom-call | flops 2013265920 | bytes 2097152 | tf_op jit(solution)/shard_map/pallas_call | solution.py:341
  23.7 0.1 collective-permute-start.4
  23.8 1.6 %collective-permute-start.5 = (bf16[128,256]{1,0:T(8,128)(2,1)S(1)}, bf16[128,256]{1,0:T(8,128)(2,1)S(1)}, u32[]{:S(2)}, u32[]{:S(2)}) collective-permute-start(bf16[128,256]{1,0:T(8,128)(2,1)S(1)} %get-tuple-element.44), channel_id=1, source_target_pairs={{0,2},{1,3},{2,0},{3,1},{4,6},{5,7},{6,4},{7,5},{8,10},{9,11},{10,... | collective-permute-start | bytes 196616 | tf_op jit(solution)/shard_map/ppermute | solution.py:32
  25.3 0.3 collective-permute-start.6
  25.6 1.7 %collective-permute-done.7 = bf16[80,16,128]{2,1,0:T(8,128)(2,1)S(1)} collective-permute-done((bf16[80,16,128]{2,1,0:T(8,128)(2,1)S(1)}, bf16[80,16,128]{2,1,0:T(8,128)(2,1)S(1)}, u32[]{:S(2)}, u32[]{:S(2)}) %collective-permute-start.7) | collective-permute-done | bytes 327712 | tf_op jit(solution)/shard_map/ppermute | solution.py:27
  27.3 1.5 %shard_map.100 = (f32[128,1280]{1,0:T(8,128)S(1)}, f32[512,256]{1,0:T(8,128)S(1)}) custom-call(bf16[4096,128]{1,0:T(8,128)(2,1)S(1)} %bitcast.15, bf16[1280,128]{1,0:T(8,128)(2,1)S(1)} %bitcast.23, bf16[4096,128]{1,0:T(8,128)(2,1)S(1)} %bitcast.20, f32[1,4096]{1,0:T(1,128)S(1)} %reshape.33.lse_ref, bf16[1024,128]{1,0:T(8,128)(2,1)S(1)} %get-tuple-element.37.keys_ref, ...), custom_call_target="tpu_custom_call" | custom-call | flops 838860800 | bytes 2097152 | tf_op jit(solution)/shard_map/pallas_call | solution.py:341
  28.8 1.6 %collective-permute-done.8 = bf16[48,16,128]{2,1,0:T(8,128)(2,1)S(1)} collective-permute-done((bf16[48,16,128]{2,1,0:T(8,128)(2,1)S(1)}, bf16[48,16,128]{2,1,0:T(8,128)(2,1)S(1)}, u32[]{:S(2)}, u32[]{:S(2)}) %collective-permute-start.8) | collective-permute-done | bytes 196640 | tf_op jit(solution)/shard_map/ppermute | solution.py:27
  30.4 1.0 %shard_map.101 = (f32[128,768]{1,0:T(8,128)S(1)}, f32[128,256]{1,0:T(8,128)S(1)}, bf16[128,256]{1,0:T(8,128)(2,1)S(1)}, bf16[128,256]{1,0:T(8,128)(2,1)S(1)}, bf16[128,256]{1,0:T(8,128)(2,1)S(1)}) custom-call(bf16[4096,128]{1,0:T(8,128)(2,1)S(1)} %bitcast.16, bf16[768,128]{1,0:T(8,128)(2,1)S(1)} %bitcast.24, bf16[4096,128]{1,0:T(8,128)(2,1)S(1)} %bitcast.21, ...), custom_call_target="tpu_custom_call" | custom-call | flops 503316480 | bytes 2097152 | tf_op jit(solution)/shard_map/pallas_call | solution.py:341
  31.4 0.1 collective-permute-start.9
  31.5 1.6 %collective-permute-start.10 = (bf16[128,256]{1,0:T(8,128)(2,1)S(1)}, bf16[128,256]{1,0:T(8,128)(2,1)S(1)}, u32[]{:S(2)}, u32[]{:S(2)}) collective-permute-start(bf16[128,256]{1,0:T(8,128)(2,1)S(1)} %get-tuple-element.58), channel_id=1, source_target_pairs={{0,2},{1,3},{2,0},{3,1},{4,6},{5,7},{6,4},{7,5},{8,10},{9,11},{10,... | collective-permute-start | bytes 196616 | tf_op jit(solution)/shard_map/ppermute | solution.py:32
  33.1 0.3 collective-permute-start.11
  33.4 1.1 %shard_map.102 = (bf16[128,256]{1,0:T(8,128)(2,1)S(1)}, bf16[4096,128]{1,0:T(8,128)(2,1)}) custom-call(f32[128,256]{1,0:T(8,128)S(1)} %get-tuple-element.42.refs_0_, bf16[128,256]{1,0:T(8,128)(2,1)S(1)} %collective-permute-done.4.refs_1_, bf16[128,256]{1,0:T(8,128)(2,1)S(1)} %collective-permute-done.5.refs_2_, ...), custom_call_target="tpu_custom_call" | custom-call | tf_op jit(solution)/shard_map/pallas_call | solution.py:271
  34.5 1.5 %collective-permute-done.10.refs_2_ = bf16[128,256]{1,0:T(8,128)(2,1)S(1)} collective-permute-done((bf16[128,256]{1,0:T(8,128)(2,1)S(1)}, bf16[128,256]{1,0:T(8,128)(2,1)S(1)}, u32[]{:S(2)}, u32[]{:S(2)}) %collective-permute-start.10) | collective-permute-done | bytes 65568 | tf_op jit(solution)/shard_map/ppermute | solution.py:32
  36.0 1.1 %collective-permute-done.11.refs_3_ = bf16[128,256]{1,0:T(8,128)(2,1)S(1)} collective-permute-done((bf16[128,256]{1,0:T(8,128)(2,1)S(1)}, bf16[128,256]{1,0:T(8,128)(2,1)S(1)}, u32[]{:S(2)}, u32[]{:S(2)}) %collective-permute-start.11) | collective-permute-done | bytes 65568 | tf_op jit(solution)/shard_map/ppermute | solution.py:32
  37.1 0.7 %shard_map.103 = (bf16[256,128]{1,0:T(8,128)(2,1)}, bf16[256,128]{1,0:T(8,128)(2,1)}) custom-call(f32[128,256]{1,0:T(8,128)S(1)} %get-tuple-element.56.refs_0_, bf16[128,256]{1,0:T(8,128)(2,1)S(1)} %collective-permute-done.9.refs_1_, bf16[128,256]{1,0:T(8,128)(2,1)S(1)} %collective-permute-done.10.refs_2_, ...), custom_call_target="tpu_custom_call" | custom-call | tf_op jit(solution)/shard_map/pallas_call | solution.py:364
  (18 shorter events, 0.1 us)
Async XLA Ops:
  0.6 1.2 %copy-start.2 = (bf16[1,256,16,128]{3,2,1,0:T(8,128)(2,1)S(1)}, bf16[1,256,16,128]{3,2,1,0:T(8,128)(2,1)}, u32[]{:S(2)}) copy-start(bf16[1,256,16,128]{3,2,1,0:T(8,128)(2,1)} %param.11) | copy-start | bytes 3145732
  1.9 12.8 %copy-start.1 = (bf16[1,256,16,128]{3,2,1,0:T(8,128)(2,1)S(1)}, bf16[1,256,16,128]{3,2,1,0:T(8,128)(2,1)}, u32[]{:S(2)}) copy-start(bf16[1,256,16,128]{3,2,1,0:T(8,128)(2,1)} %param.10) | copy-start | bytes 3145732
  1.9 6.9 %copy-start.4 = (bf16[1,256,128]{2,1,0:T(8,128)(2,1)S(1)}, bf16[1,256,128]{2,1,0:T(8,128)(2,1)}, u32[]{:S(2)}) copy-start(bf16[1,256,128]{2,1,0:T(8,128)(2,1)} %param.9) | copy-start | bytes 196612
  1.9 12.7 %collective-permute-start.3 = (bf16[64,16,128]{2,1,0:T(8,128)(2,1)S(1)}, bf16[64,16,128]{2,1,0:T(8,128)(2,1)S(1)}, u32[]{:S(2)}, u32[]{:S(2)}) collective-permute-start(bf16[64,16,128]{2,1,0:T(8,128)(2,1)S(1)} %get-tuple-element.34), channel_id=1, source_target_pairs={{0,28},{4,0},{8,4},{12,8},{16,12},{20,16},{24,20},{28,24},{1,29},{... | collective-permute-start | bytes 786440 | tf_op jit(solution)/shard_map/ppermute | solution.py:27
  8.8 3.5 %copy-start.5 = (f32[1,16,256]{2,1,0:T(8,128)S(1)}, f32[1,16,256]{2,1,0:T(8,128)}, u32[]{:S(2)}) copy-start(f32[1,16,256]{2,1,0:T(8,128)} %param.12) | copy-start | bytes 49156
  8.8 5.0 %collective-permute-start.1 = (bf16[2,256,128]{2,1,0:T(8,128)(2,1)S(1)}, bf16[2,256,128]{2,1,0:T(8,128)(2,1)S(1)}, u32[]{:S(2)}, u32[]{:S(2)}) collective-permute-start(bf16[2,256,128]{2,1,0:T(8,128)(2,1)S(1)} %constant_dynamic-update-slice_fusion.refs_0_), channel_id=1, source_target_pairs={{0,2},{1,3},{2,0},{3,1},{4,6},{5,7},{6,4},{7,5},{8,10},{9,11},{10,... | collective-permute-start | bytes 393224 | tf_op jit(solution)/shard_map/ppermute | solution.py:32
  10.4 9.9 %collective-permute-start = (bf16[64,16,128]{2,1,0:T(8,128)(2,1)S(1)}, bf16[64,16,128]{2,1,0:T(8,128)(2,1)S(1)}, u32[]{:S(2)}, u32[]{:S(2)}) collective-permute-start(bf16[64,16,128]{2,1,0:T(8,128)(2,1)S(1)} %get-tuple-element.33), channel_id=1, source_target_pairs={{0,28},{4,0},{8,4},{12,8},{16,12},{20,16},{24,20},{28,24},{1,29},{... | collective-permute-start | bytes 786440 | tf_op jit(solution)/shard_map/ppermute | solution.py:27
  11.0 16.3 %collective-permute-start.7 = (bf16[80,16,128]{2,1,0:T(8,128)(2,1)S(1)}, bf16[80,16,128]{2,1,0:T(8,128)(2,1)S(1)}, u32[]{:S(2)}, u32[]{:S(2)}) collective-permute-start(bf16[80,16,128]{2,1,0:T(8,128)(2,1)S(1)} %get-tuple-element.48), channel_id=1, source_target_pairs={{0,28},{4,0},{8,4},{12,8},{16,12},{20,16},{24,20},{28,24},{1,29},{... | collective-permute-start | bytes 983048 | tf_op jit(solution)/shard_map/ppermute | solution.py:27
  13.9 1.6 %collective-permute-start.2 = (bf16[4,256,128]{2,1,0:T(8,128)(2,1)S(1)}, bf16[4,256,128]{2,1,0:T(8,128)(2,1)S(1)}, u32[]{:S(2)}, u32[]{:S(2)}) collective-permute-start(bf16[4,256,128]{2,1,0:T(8,128)(2,1)S(1)} %shard_map.95.refs_0_), channel_id=1, source_target_pairs={{0,1},{1,0},{2,3},{3,2},{4,5},{5,4},{6,7},{7,6},{8,9},{9,8},{10,11... | collective-permute-start | bytes 786440 | tf_op jit(solution)/shard_map/ppermute | solution.py:32
  14.0 16.4 %collective-permute-start.8 = (bf16[48,16,128]{2,1,0:T(8,128)(2,1)S(1)}, bf16[48,16,128]{2,1,0:T(8,128)(2,1)S(1)}, u32[]{:S(2)}, u32[]{:S(2)}) collective-permute-start(bf16[48,16,128]{2,1,0:T(8,128)(2,1)S(1)} %get-tuple-element.52), channel_id=1, source_target_pairs={{0,28},{4,0},{8,4},{12,8},{16,12},{20,16},{24,20},{28,24},{1,29},{... | collective-permute-start | bytes 589832 | tf_op jit(solution)/shard_map/ppermute | solution.py:27
  14.7 0.8 %copy-start.3 = (s32[8]{0:T(128)S(1)}, s32[8]{0:T(128)}, u32[]{:S(2)}) copy-start(s32[8]{0:T(128)} %starts_ref.1) | copy-start | bytes 100
  14.8 1.5 %copy-start = (bf16[1,256,16,128]{3,2,1,0:T(8,128)(2,1)S(1)}, bf16[1,256,16,128]{3,2,1,0:T(8,128)(2,1)}, u32[]{:S(2)}) copy-start(bf16[1,256,16,128]{3,2,1,0:T(8,128)(2,1)} %param.7) | copy-start | bytes 3145732
  23.7 6.7 %collective-permute-start.4 = (bf16[128,256]{1,0:T(8,128)(2,1)S(1)}, bf16[128,256]{1,0:T(8,128)(2,1)S(1)}, u32[]{:S(2)}, u32[]{:S(2)}) collective-permute-start(bf16[128,256]{1,0:T(8,128)(2,1)S(1)} %get-tuple-element.43), channel_id=1, source_target_pairs={{0,1},{1,0},{2,3},{3,2},{4,5},{5,4},{6,7},{7,6},{8,9},{9,8},{10,11... | collective-permute-start | bytes 196616 | tf_op jit(solution)/shard_map/ppermute | solution.py:32
  23.8 9.6 %collective-permute-start.5 = (bf16[128,256]{1,0:T(8,128)(2,1)S(1)}, bf16[128,256]{1,0:T(8,128)(2,1)S(1)}, u32[]{:S(2)}, u32[]{:S(2)}) collective-permute-start(bf16[128,256]{1,0:T(8,128)(2,1)S(1)} %get-tuple-element.44), channel_id=1, source_target_pairs={{0,2},{1,3},{2,0},{3,1},{4,6},{5,7},{6,4},{7,5},{8,10},{9,11},{10,... | collective-permute-start | bytes 196616 | tf_op jit(solution)/shard_map/ppermute | solution.py:32
  25.3 8.0 %collective-permute-start.6 = (bf16[128,256]{1,0:T(8,128)(2,1)S(1)}, bf16[128,256]{1,0:T(8,128)(2,1)S(1)}, u32[]{:S(2)}, u32[]{:S(2)}) collective-permute-start(bf16[128,256]{1,0:T(8,128)(2,1)S(1)} %get-tuple-element.45), channel_id=1, source_target_pairs={{0,3},{1,2},{2,1},{3,0},{4,7},{5,6},{6,5},{7,4},{8,11},{9,10},{10,... | collective-permute-start | bytes 196616 | tf_op jit(solution)/shard_map/ppermute | solution.py:32
  31.4 3.1 %collective-permute-start.9 = (bf16[128,256]{1,0:T(8,128)(2,1)S(1)}, bf16[128,256]{1,0:T(8,128)(2,1)S(1)}, u32[]{:S(2)}, u32[]{:S(2)}) collective-permute-start(bf16[128,256]{1,0:T(8,128)(2,1)S(1)} %get-tuple-element.57), channel_id=1, source_target_pairs={{0,1},{1,0},{2,3},{3,2},{4,5},{5,4},{6,7},{7,6},{8,9},{9,8},{10,11... | collective-permute-start | bytes 196616 | tf_op jit(solution)/shard_map/ppermute | solution.py:32
  31.5 4.5 %collective-permute-start.10 = (bf16[128,256]{1,0:T(8,128)(2,1)S(1)}, bf16[128,256]{1,0:T(8,128)(2,1)S(1)}, u32[]{:S(2)}, u32[]{:S(2)}) collective-permute-start(bf16[128,256]{1,0:T(8,128)(2,1)S(1)} %get-tuple-element.58), channel_id=1, source_target_pairs={{0,2},{1,3},{2,0},{3,1},{4,6},{5,7},{6,4},{7,5},{8,10},{9,11},{10,... | collective-permute-start | bytes 196616 | tf_op jit(solution)/shard_map/ppermute | solution.py:32
  33.1 4.0 %collective-permute-start.11 = (bf16[128,256]{1,0:T(8,128)(2,1)S(1)}, bf16[128,256]{1,0:T(8,128)(2,1)S(1)}, u32[]{:S(2)}, u32[]{:S(2)}) collective-permute-start(bf16[128,256]{1,0:T(8,128)(2,1)S(1)} %get-tuple-element.59), channel_id=1, source_target_pairs={{0,3},{1,2},{2,1},{3,0},{4,7},{5,6},{6,5},{7,4},{8,11},{9,10},{10,... | collective-permute-start | bytes 196616 | tf_op jit(solution)/shard_map/ppermute | solution.py:32

commit v4 on v3

--- a/solution.py
+++ b/solution.py
@@ -217,6 +217,37 @@
         target[:, head_size:] = total_ref[rows, head_size:].astype(target.dtype)
 
 
+def hand_half(half, count, span_rows, places_ref, total_ref, kept_ref, send_ref):
+    head_size = total_ref.shape[1] // 2
+    scale = head_size**-0.5
+    for code in range(count):
+        rows = pl.ds(place_of(places_ref, code, half), span_rows)
+        target = send_ref if code % 2 else kept_ref
+        target[code // 2, :, :head_size] = (total_ref[rows, :head_size] * scale).astype(target.dtype)
+        target[code // 2, :, head_size:] = total_ref[rows, head_size:].astype(target.dtype)
+
+
+def halve_kernel(kept_in_ref, got_ref, kept_ref, send_ref):
+    for i in range(kept_in_ref.shape[0]):
+        total = kept_in_ref[i] + got_ref[i].astype(jnp.float32)
+        target = send_ref if i % 2 else kept_ref
+        target[i // 2] = total.astype(target.dtype)
+
+
+def halve(kept, got):
+    shape = (kept.shape[0] // 2, *kept.shape[1:])
+    return pl.pallas_call(
+        halve_kernel,
+        out_shape=(
+            jax.ShapeDtypeStruct(shape, jnp.float32),
+            jax.ShapeDtypeStruct(shape, jnp.bfloat16),
+        ),
+        in_specs=[WHOLE] * 2,
+        out_specs=(WHOLE,) * 2,
+        compiler_params=params(),
+    )(kept, got)
+
+
 def add_terms(term_refs):
     total = term_refs[0][...]
     for term_ref in term_refs[1:]:
@@ -240,13 +271,14 @@
         chunk, heads, span_rows, places_ref, q_ref, g_ref, o_ref, lse_ref, keys_ref, values_ref,
         keys_t_ref, total_ref, dq_ref,
     )
-    if hands_out:
+    if is_last:
+        hand_half(chunk[0], count, span_rows, places_ref, total_ref, *handed)
+    elif hands_out:
         hand_out(chunk[0], count, span_rows, places_ref, total_ref, handed[0], handed[1:])
 
 
-def add_kernel(count, span_rows, head_size, *refs):
-    term_refs, upper_ref, (key_ref, value_ref) = refs[:count], refs[count], refs[count + 1 :]
-    lower = add_terms(term_refs).astype(jnp.bfloat16)
+def add_kernel(span_rows, head_size, kept_ref, got_ref, upper_ref, key_ref, value_ref):
+    lower = (kept_ref[0] + got_ref[0].astype(jnp.float32)).astype(jnp.bfloat16)
     for out_ref, columns in ((key_ref, slice(0, head_size)), (value_ref, slice(head_size, None))):
         out_ref[:span_rows, :] = lower[:, columns]
         out_ref[span_rows:, :] = upper_ref[:, columns]
@@ -320,7 +352,7 @@
         rows = tokens * heads
         is_first, is_last = number == 0, number == len(chunks) - 1
         hands_out = chunk[1] + tokens == span_rows
-        after = received[:2] if is_last else []
+        after = received if is_last else []
         if is_last:
             upper_terms = received
         grad = grads[number].reshape(rows, head_size)
@@ -334,7 +366,10 @@
         out_shape = [jax.ShapeDtypeStruct((head_size, rows), jnp.float32)]
         if not is_last:
             out_shape.append(jax.ShapeDtypeStruct(total_shape, jnp.float32))
-        if hands_out:
+        if is_last:
+            out_shape.append(jax.ShapeDtypeStruct((count // 2, *span_wide), jnp.float32))
+            out_shape.append(jax.ShapeDtypeStruct((count // 2, *span_wide), jnp.bfloat16))
+        elif hands_out:
             out_shape.append(jax.ShapeDtypeStruct(span_wide, jnp.float32))
             out_shape += [jax.ShapeDtypeStruct(span_wide, jnp.bfloat16)] * (count - 1)
         pairs = rows * (3 * total // 4 if half == 1 else total // 4)
@@ -354,20 +389,26 @@
         )(*operands)
         dq_parts.append(dq)
         running = [] if is_last else [handed.pop(0)]
-        if hands_out:
-            sends = list(enumerate(handed[1:], start=1))
-            received = [with_partner(send, "ctx", step) for step, send in reversed(sends)]
-            received = [handed[0]] + received[::-1]
+        if is_last:
+            kept, send = handed
+            got, step = with_partner(send, "ctx", 1), 2
+            while step < count:
+                kept, send = halve(kept, got)
+                got, step = with_partner(send, "ctx", step), 2 * step
+        elif hands_out:
+            received = [handed[0]] + [
+                with_partner(send, "ctx", step) for step, send in enumerate(handed[1:], start=1)
+            ]
 
     places = [(half * span_rows + first) * heads for half, first, _ in chunks]
     upper_sum, dq = finish(upper_terms, dq_parts, places, q_flat.shape)
     key_out, value_out = pl.pallas_call(
-        functools.partial(add_kernel, count, span_rows, head_size),
+        functools.partial(add_kernel, span_rows, head_size),
         out_shape=(jax.ShapeDtypeStruct((row_count, head_size), jnp.bfloat16),) * 2,
-        in_specs=[WHOLE] * (count + 1),
+        in_specs=[WHOLE] * 3,
         out_specs=(WHOLE,) * 2,
         compiler_params=params(),
-    )(*received, upper_sum)
+    )(kept, got, upper_sum)
     return (dq.reshape(queries.shape), key_out[None], value_out[None])
 
 

time: 38.3 us -> 38.3 us (level)
    ppermute x8 -> x7, starting transfers between devices: 5.52 us -> 5.76 us  [with_partner(): return lax.ppermute(shard, axis, [(i, i ^ step) for i in range(length)])]
    ppermute x8 -> x7, waiting for transfers between devices: 4.61 us -> 4.59 us  [with_partner(): return lax.ppermute(shard, axis, [(i, i ^ step) for i in range(length)])]
  transfers between devices with their start and end apart: 12 -> 11, of which waited for: 8 -> 8; matrix products, arithmetic and copies ran while one was open for 3% -> 3% of each run, Pallas kernels for 30% -> 26%
where the time goes in v4:
time: 38.3 us; the launch traced here: 38.1 us
  starting transfers between devices  14.3 us (37%)
  Pallas kernels  11.9 us (31%)
  waiting for transfers between devices  8.81 us (23%)
  local copies, waits for them, and re-layouts  2.31 us (6%)
  between operations  0.78 us (2%)
    pallas_call x4, Pallas kernels, body(): pl.pallas_call(functools.partial(chunk_kernel, chunk, heads, span_rows, c...  9.05 us
    ppermute x4, starting transfers between devices, from_behind(): lax.ppermute(shard, axis, [(i, (i + by) % length) for i in range(length)])  8.53 us
    ppermute x7, starting transfers between devices, with_partner(): return lax.ppermute(shard, axis, [(i, i ^ step) for i in range(length)])  5.76 us
    ppermute x7, waiting for transfers between devices, with_partner(): return lax.ppermute(shard, axis, [(i, i ^ step) for i in range(length)])  4.59 us
    ppermute x4, waiting for transfers between devices, from_behind(): lax.ppermute(shard, axis, [(i, (i + by) % length) for i in range(length)])  4.21 us
    unnamed x13, local copies, waits for them, and re-layouts  2.09 us
    pallas_call x1, Pallas kernels, finish(): pl.pallas_call(functools.partial(finish_kernel, len(terms), places), out_...  1.13 us
    pallas_call x1, Pallas kernels, sort_keys(): pl.pallas_call(functools.partial(sort_keys_kernel, codes, span_rows, head...  0.79 us
  transfers between devices with their start and end apart: 11, of which 8 were waited for; matrix products, arithmetic and copies ran while one was open for 3% of the time, Pallas kernels for 26%

profile of v4, /device:TPU:0, one launch (start us, length us, event | category | flops | bytes accessed | tf_op | source)
XLA Modules:
  0.0 38.1 jit_solution(10546332282425953548)
XLA Ops:
  0.6 1.2 %copy-done.2 = bf16[1,256,16,128]{3,2,1,0:T(8,128)(2,1)S(1)} copy-done((bf16[1,256,16,128]{3,2,1,0:T(8,128)(2,1)S(1)}, bf16[1,256,16,128]{3,2,1,0:T(8,128)(2,1)}, u32[]{:S(2)}) %copy-start.2) | copy-done | bytes 1048600
  1.9 0.1 shard_map.94
  1.9 6.0 %collective-permute-start.3 = (bf16[64,16,128]{2,1,0:T(8,128)(2,1)S(1)}, bf16[64,16,128]{2,1,0:T(8,128)(2,1)S(1)}, u32[]{:S(2)}, u32[]{:S(2)}) collective-permute-start(bf16[64,16,128]{2,1,0:T(8,128)(2,1)S(1)} %get-tuple-element.34), channel_id=1, source_target_pairs={{0,28},{4,0},{8,4},{12,8},{16,12},{20,16},{24,20},{28,24},{1,29},{... | collective-permute-start | bytes 786440 | tf_op jit(solution)/shard_map/ppermute | solution.py:27
  8.0 0.8 %constant_dynamic-update-slice_fusion.1 = bf16[2,256,128]{2,1,0:T(8,128)(2,1)S(1)} fusion(bf16[1,256,128]{2,1,0:T(8,128)(2,1)} %param.8), kind=kLoop, calls=%fused_computation.1 | loop fusion | bytes 131072
  8.8 1.6 %collective-permute-start.1 = (bf16[2,256,128]{2,1,0:T(8,128)(2,1)S(1)}, bf16[2,256,128]{2,1,0:T(8,128)(2,1)S(1)}, u32[]{:S(2)}, u32[]{:S(2)}) collective-permute-start(bf16[2,256,128]{2,1,0:T(8,128)(2,1)S(1)} %constant_dynamic-update-slice_fusion.refs_0_), channel_id=1, source_target_pairs={{0,2},{1,3},{2,0},{3,1},{4,6},{5,7},{6,4},{7,5},{8,10},{9,11},{10,... | collective-permute-start | bytes 393224 | tf_op jit(solution)/shard_map/ppermute | solution.py:32
  10.4 0.5 %collective-permute-start = (bf16[64,16,128]{2,1,0:T(8,128)(2,1)S(1)}, bf16[64,16,128]{2,1,0:T(8,128)(2,1)S(1)}, u32[]{:S(2)}, u32[]{:S(2)}) collective-permute-start(bf16[64,16,128]{2,1,0:T(8,128)(2,1)S(1)} %get-tuple-element.33), channel_id=1, source_target_pairs={{0,28},{4,0},{8,4},{12,8},{16,12},{20,16},{24,20},{28,24},{1,29},{... | collective-permute-start | bytes 786440 | tf_op jit(solution)/shard_map/ppermute | solution.py:27
  11.0 1.4 %collective-permute-start.7 = (bf16[80,16,128]{2,1,0:T(8,128)(2,1)S(1)}, bf16[80,16,128]{2,1,0:T(8,128)(2,1)S(1)}, u32[]{:S(2)}, u32[]{:S(2)}) collective-permute-start(bf16[80,16,128]{2,1,0:T(8,128)(2,1)S(1)} %get-tuple-element.48), channel_id=1, source_target_pairs={{0,28},{4,0},{8,4},{12,8},{16,12},{20,16},{24,20},{28,24},{1,29},{... | collective-permute-start | bytes 983048 | tf_op jit(solution)/shard_map/ppermute | solution.py:27
  12.3 0.1 copy.11
  12.4 0.1 reshape.33.lse_ref
  12.6 1.3 %collective-permute-done.1.refs_1_ = bf16[2,256,128]{2,1,0:T(8,128)(2,1)S(1)} collective-permute-done((bf16[2,256,128]{2,1,0:T(8,128)(2,1)S(1)}, bf16[2,256,128]{2,1,0:T(8,128)(2,1)S(1)}, u32[]{:S(2)}, u32[]{:S(2)}) %collective-permute-start.1) | collective-permute-done | bytes 131104 | tf_op jit(solution)/shard_map/ppermute | solution.py:32
  13.9 0.1 collective-permute-start.2
  14.0 0.6 %collective-permute-start.8 = (bf16[48,16,128]{2,1,0:T(8,128)(2,1)S(1)}, bf16[48,16,128]{2,1,0:T(8,128)(2,1)S(1)}, u32[]{:S(2)}, u32[]{:S(2)}) collective-permute-start(bf16[48,16,128]{2,1,0:T(8,128)(2,1)S(1)} %get-tuple-element.52), channel_id=1, source_target_pairs={{0,28},{4,0},{8,4},{12,8},{16,12},{20,16},{24,20},{28,24},{1,29},{... | collective-permute-start | bytes 589832 | tf_op jit(solution)/shard_map/ppermute | solution.py:27
  14.6 0.1 collective-permute-done.3
  14.7 0.1 shard_map.97.g_ref
  14.8 0.7 %collective-permute-done.2.refs_1_ = bf16[4,256,128]{2,1,0:T(8,128)(2,1)S(1)} collective-permute-done((bf16[4,256,128]{2,1,0:T(8,128)(2,1)S(1)}, bf16[4,256,128]{2,1,0:T(8,128)(2,1)S(1)}, u32[]{:S(2)}, u32[]{:S(2)}) %collective-permute-start.2) | collective-permute-done | bytes 262176 | tf_op jit(solution)/shard_map/ppermute | solution.py:32
  15.5 0.8 %shard_map.96 = (bf16[1024,128]{1,0:T(8,128)(2,1)S(1)}, bf16[1024,256]{1,0:T(8,128)(2,1)S(1)}, bf16[128,1024]{1,0:T(8,128)(2,1)S(1)}, f32[8,128]{1,0:T(8,128)S(1)}) custom-call(s32[8]{0:T(128)S(1)} %copy-done.3, bf16[4,256,128]{2,1,0:T(8,128)(2,1)S(1)} %shard_map.95.refs_0_, bf16[4,256,128]{2,1,0:T(8,128)(2,1)S(1)} %collective-permute-done.2.refs_1_), custom_call_target="tpu_custom_call" | custom-call | flops 1000000000 | bytes 1048576 | tf_op jit(solution)/shard_map/pallas_call | solution.py:137
  16.3 3.1 %shard_map.98 = (f32[128,1024]{1,0:T(8,128)S(1)}, f32[1024,256]{1,0:T(8,128)S(1)}) custom-call(bf16[4096,128]{1,0:T(8,128)(2,1)S(1)} %bitcast.13, bf16[1024,256]{1,0:T(8,128)(2,1)S(1)} %shard_map.97.g_ref, bf16[4096,128]{1,0:T(8,128)(2,1)S(1)} %bitcast.18, f32[1,4096]{1,0:T(1,128)S(1)} %reshape.33.lse_ref, bf16[1024,128]{1,0:T(8,128)(2,1)S(1)} %get-tuple-element.37.keys_ref, ...), custom_call_target="tpu_custom_call" | custom-call | flops 2013265920 | bytes 2097152 | tf_op jit(solution)/shard_map/pallas_call | solution.py:376
  19.5 0.8 %collective-permute-done = bf16[64,16,128]{2,1,0:T(8,128)(2,1)S(1)} collective-permute-done((bf16[64,16,128]{2,1,0:T(8,128)(2,1)S(1)}, bf16[64,16,128]{2,1,0:T(8,128)(2,1)S(1)}, u32[]{:S(2)}, u32[]{:S(2)}) %collective-permute-start) | collective-permute-done | bytes 262176 | tf_op jit(solution)/shard_map/ppermute | solution.py:27
  20.3 3.4 %shard_map.99 = (f32[128,1024]{1,0:T(8,128)S(1)}, f32[1024,256]{1,0:T(8,128)S(1)}, f32[128,256]{1,0:T(8,128)S(1)}, bf16[128,256]{1,0:T(8,128)(2,1)S(1)}, bf16[12...) custom-call(bf16[4096,128]{1,0:T(8,128)(2,1)S(1)} %bitcast.14, bf16[1024,128]{1,0:T(8,128)(2,1)S(1)} %bitcast.25, ...), custom_call_target="tpu_custom_call" | custom-call | flops 2013265920 | bytes 2097152 | tf_op jit(solution)/shard_map/pallas_call | solution.py:376
  23.7 0.1 collective-permute-start.4
  23.8 0.9 %collective-permute-start.5 = (bf16[128,256]{1,0:T(8,128)(2,1)S(1)}, bf16[128,256]{1,0:T(8,128)(2,1)S(1)}, u32[]{:S(2)}, u32[]{:S(2)}) collective-permute-start(bf16[128,256]{1,0:T(8,128)(2,1)S(1)} %get-tuple-element.44), channel_id=1, source_target_pairs={{0,2},{1,3},{2,0},{3,1},{4,6},{5,7},{6,4},{7,5},{8,10},{9,11},{10,... | collective-permute-start | bytes 196616 | tf_op jit(solution)/shard_map/ppermute | solution.py:32
  24.7 0.9 %collective-permute-start.6 = (bf16[128,256]{1,0:T(8,128)(2,1)S(1)}, bf16[128,256]{1,0:T(8,128)(2,1)S(1)}, u32[]{:S(2)}, u32[]{:S(2)}) collective-permute-start(bf16[128,256]{1,0:T(8,128)(2,1)S(1)} %get-tuple-element.45), channel_id=1, source_target_pairs={{0,3},{1,2},{2,1},{3,0},{4,7},{5,6},{6,5},{7,4},{8,11},{9,10},{10,... | collective-permute-start | bytes 196616 | tf_op jit(solution)/shard_map/ppermute | solution.py:32
  25.6 1.7 %collective-permute-done.7 = bf16[80,16,128]{2,1,0:T(8,128)(2,1)S(1)} collective-permute-done((bf16[80,16,128]{2,1,0:T(8,128)(2,1)S(1)}, bf16[80,16,128]{2,1,0:T(8,128)(2,1)S(1)}, u32[]{:S(2)}, u32[]{:S(2)}) %collective-permute-start.7) | collective-permute-done | bytes 327712 | tf_op jit(solution)/shard_map/ppermute | solution.py:27
  27.3 1.5 %shard_map.100 = (f32[128,1280]{1,0:T(8,128)S(1)}, f32[512,256]{1,0:T(8,128)S(1)}) custom-call(bf16[4096,128]{1,0:T(8,128)(2,1)S(1)} %bitcast.15, bf16[1280,128]{1,0:T(8,128)(2,1)S(1)} %bitcast.23, bf16[4096,128]{1,0:T(8,128)(2,1)S(1)} %bitcast.20, f32[1,4096]{1,0:T(1,128)S(1)} %reshape.33.lse_ref, bf16[1024,128]{1,0:T(8,128)(2,1)S(1)} %get-tuple-element.37.keys_ref, ...), custom_call_target="tpu_custom_call" | custom-call | flops 838860800 | bytes 2097152 | tf_op jit(solution)/shard_map/pallas_call | solution.py:376
  28.8 1.6 %collective-permute-done.8 = bf16[48,16,128]{2,1,0:T(8,128)(2,1)S(1)} collective-permute-done((bf16[48,16,128]{2,1,0:T(8,128)(2,1)S(1)}, bf16[48,16,128]{2,1,0:T(8,128)(2,1)S(1)}, u32[]{:S(2)}, u32[]{:S(2)}) %collective-permute-start.8) | collective-permute-done | bytes 196640 | tf_op jit(solution)/shard_map/ppermute | solution.py:27
  30.4 1.0 %shard_map.101 = (f32[128,768]{1,0:T(8,128)S(1)}, f32[2,128,256]{2,1,0:T(8,128)S(1)}, bf16[2,128,256]{2,1,0:T(8,128)(2,1)S(1)}) custom-call(bf16[4096,128]{1,0:T(8,128)(2,1)S(1)} %bitcast.16, bf16[768,128]{1,0:T(8,128)(2,1)S(1)} %bitcast.24, bf16[4096,128]{1,0:T(8,128)(2,1)S(1)} %bitcast.21, f32[1,4096]{1,0:T(1,128)S(1)} %reshape.33.lse_ref, ...), custom_call_target="tpu_custom_call" | custom-call | flops 503316480 | bytes 2097152 | tf_op jit(solution)/shard_map/pallas_call | solution.py:376
  31.4 0.1 collective-permute-start.9
  31.5 1.3 %collective-permute-done.9.got_ref = bf16[2,128,256]{2,1,0:T(8,128)(2,1)S(1)} collective-permute-done((bf16[2,128,256]{2,1,0:T(8,128)(2,1)S(1)}, bf16[2,128,256]{2,1,0:T(8,128)(2,1)S(1)}, u32[]{:S(2)}, u32[]{:S(2)}) %collective-permute-start.9) | collective-permute-done | bytes 131104 | tf_op jit(solution)/shard_map/ppermute | solution.py:32
  32.9 2.1 %collective-permute-start.10 = (bf16[1,128,256]{2,1,0:T(8,128)(2,1)S(1)}, bf16[1,128,256]{2,1,0:T(8,128)(2,1)S(1)}, u32[]{:S(2)}, u32[]{:S(2)}) collective-permute-start(bf16[1,128,256]{2,1,0:T(8,128)(2,1)S(1)} %get-tuple-element.59), channel_id=1, source_target_pairs={{0,2},{1,3},{2,0},{3,1},{4,6},{5,7},{6,4},{7,5},{8,10},{9,11},{10,... | collective-permute-start | bytes 196616 | tf_op jit(solution)/shard_map/ppermute | solution.py:32
  35.0 1.1 %shard_map.102 = (bf16[128,256]{1,0:T(8,128)(2,1)S(1)}, bf16[4096,128]{1,0:T(8,128)(2,1)}) custom-call(f32[128,256]{1,0:T(8,128)S(1)} %get-tuple-element.42.refs_0_, bf16[128,256]{1,0:T(8,128)(2,1)S(1)} %collective-permute-done.4.refs_1_, bf16[128,256]{1,0:T(8,128)(2,1)S(1)} %collective-permute-done.5.refs_2_, ...), custom_call_target="tpu_custom_call" | custom-call | tf_op jit(solution)/shard_map/pallas_call | solution.py:303
  36.1 1.3 %collective-permute-done.10.got_ref = bf16[1,128,256]{2,1,0:T(8,128)(2,1)S(1)} collective-permute-done((bf16[1,128,256]{2,1,0:T(8,128)(2,1)S(1)}, bf16[1,128,256]{2,1,0:T(8,128)(2,1)S(1)}, u32[]{:S(2)}, u32[]{:S(2)}) %collective-permute-start.10) | collective-permute-done | bytes 65568 | tf_op jit(solution)/shard_map/ppermute | solution.py:32
  37.4 0.7 %shard_map.104 = (bf16[256,128]{1,0:T(8,128)(2,1)}, bf16[256,128]{1,0:T(8,128)(2,1)}) custom-call(f32[1,128,256]{2,1,0:T(8,128)S(1)} %get-tuple-element.58.kept_ref, bf16[1,128,256]{2,1,0:T(8,128)(2,1)S(1)} %collective-permute-done.10.got_ref, bf16[128,256]{1,0:T(8,128)(2,1)S(1)} %get-tuple-element.60.upper_ref), custom_call_target="tpu_custom_call" | custom-call | tf_op jit(solution)/shard_map/pallas_call | solution.py:405
  (17 shorter events, 0.1 us)
Async XLA Ops:
  0.6 1.2 %copy-start.2 = (bf16[1,256,16,128]{3,2,1,0:T(8,128)(2,1)S(1)}, bf16[1,256,16,128]{3,2,1,0:T(8,128)(2,1)}, u32[]{:S(2)}) copy-start(bf16[1,256,16,128]{3,2,1,0:T(8,128)(2,1)} %param.11) | copy-start | bytes 3145732
  1.9 12.8 %copy-start.1 = (bf16[1,256,16,128]{3,2,1,0:T(8,128)(2,1)S(1)}, bf16[1,256,16,128]{3,2,1,0:T(8,128)(2,1)}, u32[]{:S(2)}) copy-start(bf16[1,256,16,128]{3,2,1,0:T(8,128)(2,1)} %param.10) | copy-start | bytes 3145732
  1.9 6.9 %copy-start.4 = (bf16[1,256,128]{2,1,0:T(8,128)(2,1)S(1)}, bf16[1,256,128]{2,1,0:T(8,128)(2,1)}, u32[]{:S(2)}) copy-start(bf16[1,256,128]{2,1,0:T(8,128)(2,1)} %param.9) | copy-start | bytes 196612
  1.9 12.7 %collective-permute-start.3 = (bf16[64,16,128]{2,1,0:T(8,128)(2,1)S(1)}, bf16[64,16,128]{2,1,0:T(8,128)(2,1)S(1)}, u32[]{:S(2)}, u32[]{:S(2)}) collective-permute-start(bf16[64,16,128]{2,1,0:T(8,128)(2,1)S(1)} %get-tuple-element.34), channel_id=1, source_target_pairs={{0,28},{4,0},{8,4},{12,8},{16,12},{20,16},{24,20},{28,24},{1,29},{... | collective-permute-start | bytes 786440 | tf_op jit(solution)/shard_map/ppermute | solution.py:27
  8.8 3.5 %copy-start.5 = (f32[1,16,256]{2,1,0:T(8,128)S(1)}, f32[1,16,256]{2,1,0:T(8,128)}, u32[]{:S(2)}) copy-start(f32[1,16,256]{2,1,0:T(8,128)} %param.12) | copy-start | bytes 49156
  8.8 5.0 %collective-permute-start.1 = (bf16[2,256,128]{2,1,0:T(8,128)(2,1)S(1)}, bf16[2,256,128]{2,1,0:T(8,128)(2,1)S(1)}, u32[]{:S(2)}, u32[]{:S(2)}) collective-permute-start(bf16[2,256,128]{2,1,0:T(8,128)(2,1)S(1)} %constant_dynamic-update-slice_fusion.refs_0_), channel_id=1, source_target_pairs={{0,2},{1,3},{2,0},{3,1},{4,6},{5,7},{6,4},{7,5},{8,10},{9,11},{10,... | collective-permute-start | bytes 393224 | tf_op jit(solution)/shard_map/ppermute | solution.py:32
  10.4 9.9 %collective-permute-start = (bf16[64,16,128]{2,1,0:T(8,128)(2,1)S(1)}, bf16[64,16,128]{2,1,0:T(8,128)(2,1)S(1)}, u32[]{:S(2)}, u32[]{:S(2)}) collective-permute-start(bf16[64,16,128]{2,1,0:T(8,128)(2,1)S(1)} %get-tuple-element.33), channel_id=1, source_target_pairs={{0,28},{4,0},{8,4},{12,8},{16,12},{20,16},{24,20},{28,24},{1,29},{... | collective-permute-start | bytes 786440 | tf_op jit(solution)/shard_map/ppermute | solution.py:27
  11.0 16.3 %collective-permute-start.7 = (bf16[80,16,128]{2,1,0:T(8,128)(2,1)S(1)}, bf16[80,16,128]{2,1,0:T(8,128)(2,1)S(1)}, u32[]{:S(2)}, u32[]{:S(2)}) collective-permute-start(bf16[80,16,128]{2,1,0:T(8,128)(2,1)S(1)} %get-tuple-element.48), channel_id=1, source_target_pairs={{0,28},{4,0},{8,4},{12,8},{16,12},{20,16},{24,20},{28,24},{1,29},{... | collective-permute-start | bytes 983048 | tf_op jit(solution)/shard_map/ppermute | solution.py:27
  13.9 1.6 %collective-permute-start.2 = (bf16[4,256,128]{2,1,0:T(8,128)(2,1)S(1)}, bf16[4,256,128]{2,1,0:T(8,128)(2,1)S(1)}, u32[]{:S(2)}, u32[]{:S(2)}) collective-permute-start(bf16[4,256,128]{2,1,0:T(8,128)(2,1)S(1)} %shard_map.95.refs_0_), channel_id=1, source_target_pairs={{0,1},{1,0},{2,3},{3,2},{4,5},{5,4},{6,7},{7,6},{8,9},{9,8},{10,11... | collective-permute-start | bytes 786440 | tf_op jit(solution)/shard_map/ppermute | solution.py:32
  14.0 16.4 %collective-permute-start.8 = (bf16[48,16,128]{2,1,0:T(8,128)(2,1)S(1)}, bf16[48,16,128]{2,1,0:T(8,128)(2,1)S(1)}, u32[]{:S(2)}, u32[]{:S(2)}) collective-permute-start(bf16[48,16,128]{2,1,0:T(8,128)(2,1)S(1)} %get-tuple-element.52), channel_id=1, source_target_pairs={{0,28},{4,0},{8,4},{12,8},{16,12},{20,16},{24,20},{28,24},{1,29},{... | collective-permute-start | bytes 589832 | tf_op jit(solution)/shard_map/ppermute | solution.py:27
  14.7 0.8 %copy-start.3 = (s32[8]{0:T(128)S(1)}, s32[8]{0:T(128)}, u32[]{:S(2)}) copy-start(s32[8]{0:T(128)} %starts_ref.1) | copy-start | bytes 100
  14.8 1.5 %copy-start = (bf16[1,256,16,128]{3,2,1,0:T(8,128)(2,1)S(1)}, bf16[1,256,16,128]{3,2,1,0:T(8,128)(2,1)}, u32[]{:S(2)}) copy-start(bf16[1,256,16,128]{3,2,1,0:T(8,128)(2,1)} %param.7) | copy-start | bytes 3145732
  23.7 6.7 %collective-permute-start.4 = (bf16[128,256]{1,0:T(8,128)(2,1)S(1)}, bf16[128,256]{1,0:T(8,128)(2,1)S(1)}, u32[]{:S(2)}, u32[]{:S(2)}) collective-permute-start(bf16[128,256]{1,0:T(8,128)(2,1)S(1)} %get-tuple-element.43), channel_id=1, source_target_pairs={{0,1},{1,0},{2,3},{3,2},{4,5},{5,4},{6,7},{7,6},{8,9},{9,8},{10,11... | collective-permute-start | bytes 196616 | tf_op jit(solution)/shard_map/ppermute | solution.py:32
  23.8 6.6 %collective-permute-start.5 = (bf16[128,256]{1,0:T(8,128)(2,1)S(1)}, bf16[128,256]{1,0:T(8,128)(2,1)S(1)}, u32[]{:S(2)}, u32[]{:S(2)}) collective-permute-start(bf16[128,256]{1,0:T(8,128)(2,1)S(1)} %get-tuple-element.44), channel_id=1, source_target_pairs={{0,2},{1,3},{2,0},{3,1},{4,6},{5,7},{6,4},{7,5},{8,10},{9,11},{10,... | collective-permute-start | bytes 196616 | tf_op jit(solution)/shard_map/ppermute | solution.py:32
  24.7 5.7 %collective-permute-start.6 = (bf16[128,256]{1,0:T(8,128)(2,1)S(1)}, bf16[128,256]{1,0:T(8,128)(2,1)S(1)}, u32[]{:S(2)}, u32[]{:S(2)}) collective-permute-start(bf16[128,256]{1,0:T(8,128)(2,1)S(1)} %get-tuple-element.45), channel_id=1, source_target_pairs={{0,3},{1,2},{2,1},{3,0},{4,7},{5,6},{6,5},{7,4},{8,11},{9,10},{10,... | collective-permute-start | bytes 196616 | tf_op jit(solution)/shard_map/ppermute | solution.py:32
  31.4 1.4 %collective-permute-start.9 = (bf16[2,128,256]{2,1,0:T(8,128)(2,1)S(1)}, bf16[2,128,256]{2,1,0:T(8,128)(2,1)S(1)}, u32[]{:S(2)}, u32[]{:S(2)}) collective-permute-start(bf16[2,128,256]{2,1,0:T(8,128)(2,1)S(1)} %get-tuple-element.57), channel_id=1, source_target_pairs={{0,1},{1,0},{2,3},{3,2},{4,5},{5,4},{6,7},{7,6},{8,9},{9,8},{10,11... | collective-permute-start | bytes 393224 | tf_op jit(solution)/shard_map/ppermute | solution.py:32
  32.9 4.5 %collective-permute-start.10 = (bf16[1,128,256]{2,1,0:T(8,128)(2,1)S(1)}, bf16[1,128,256]{2,1,0:T(8,128)(2,1)S(1)}, u32[]{:S(2)}, u32[]{:S(2)}) collective-permute-start(bf16[1,128,256]{2,1,0:T(8,128)(2,1)S(1)} %get-tuple-element.59), channel_id=1, source_target_pairs={{0,2},{1,3},{2,0},{3,1},{4,6},{5,7},{6,4},{7,5},{8,10},{9,11},{10,... | collective-permute-start | bytes 196616 | tf_op jit(solution)/shard_map/ppermute | solution.py:32
